TPU v7x, 512 devices: a whole 4x8x8 slice. The times are simulated.
512 devices in a mesh: dp: 128 (over x, z, y_lo), tensor: 4 (over y_hi, core).
Axes of the slice: x: 4, y: 8 (y_hi: 2, y_lo: 4; y = y_hi * 4 + y_lo), z: 8, core: 2. Of those that a mesh axis runs over, the one named last changes fastest.
Arguments:
- images: bfloat16 [32768, 1152], P('dp'), may hold values from -6 to 6
- layer_norm_gain: float32 [1152], replicated, may hold values from 0.5 to 1.5
- hidden_weight: bfloat16 [1152, 4304], P('dp', 'tensor'), may hold values from -0.1875 to 0.1875
- output_weight: bfloat16 [4304, 1152], P('tensor', 'dp'), may hold values from -0.09375 to 0.09375
- text: bfloat16 [32768, 1152], P(('dp', 'tensor')), may hold values from -6 to 6
Outputs:
- images_gradient: float32 [32768, 1152], P('dp')
- grad_text: float32 [32768, 1152], P(('dp', 'tensor'))
All inputs are finite; a program needn't handle non-finite values.
Results may differ from a plain program's by a relative error of at most 0.006.
Values may be sent and summed in bfloat16 or wider, within the bound.
A program may use at most 64 MiB of HBM per device.

v0:
```python
import jax
import jax.numpy as jnp
from jax import lax
from jax.sharding import PartitionSpec as P

HOPS = 8


SCALE_LOGIT = 10.0
BIAS_LOGIT = -3.0
EPS = 1e-06


def from_behind(array, axis, by):
    peers = lax.axis_size(axis)
    return lax.ppermute(array, axis, [(i, (i + by) % peers) for i in range(peers)])


def gelu_tanh(values):
    return jax.nn.gelu(values, approximate=True)


def unit_rows(values):
    row_norm = jnp.sqrt(jnp.sum(values * values, axis=-1, keepdims=True) + EPS)
    return (values / row_norm, row_norm)


def contract_last(left, right):
    return lax.dot_general(
        left, right, (((1,), (1,)), ((), ())), preferred_element_type=jnp.float32
    )


def shards(images, layer_norm_gain, hidden_weight, output_weight, text):
    row_count = images.shape[0]
    quarter = text.shape[0]
    half_hops = HOPS // 2
    member = lax.axis_index("tensor")
    features = images.astype(jnp.float32)
    feature_mean = jnp.mean(features, axis=1, keepdims=True)
    mean_shifted_input = features - feature_mean
    variance = jnp.mean(mean_shifted_input * mean_shifted_input, axis=1, keepdims=True)
    reciprocal_deviation = 1.0 / jnp.sqrt(variance + EPS)
    standardized_input = mean_shifted_input * reciprocal_deviation
    normalized_input = (standardized_input * layer_norm_gain).astype(jnp.bfloat16)
    hidden_full, output_full = (
        lax.all_gather(hidden_weight, "dp", axis=0, tiled=True),
        lax.all_gather(output_weight, "dp", axis=1, tiled=True),
    )
    preact = jnp.dot(normalized_input, hidden_full, preferred_element_type=jnp.float32)
    activated = gelu_tanh(preact).astype(jnp.bfloat16)
    head_terms = jnp.dot(activated, output_full, preferred_element_type=jnp.float32)
    head_out = features + lax.psum(head_terms, "tensor")
    image_f, image_norm = unit_rows(head_out)
    image_unit = image_f.astype(jnp.bfloat16)
    text_f, text_norm = unit_rows(text.astype(jnp.float32))
    text_unit = text_f.astype(jnp.bfloat16)
    row_ids = lax.broadcasted_iota(jnp.int32, (row_count, quarter), 0)
    col_ids = lax.broadcasted_iota(jnp.int32, (row_count, quarter), 1)
    own_mark = (row_ids == col_ids + member * quarter).astype(jnp.float32)
    no_mark = jnp.zeros((row_count, quarter), jnp.float32)
    text_block = from_behind(text_unit, "dp", half_hops)
    grad_image = jnp.zeros((row_count, images.shape[1]), jnp.float32)
    carried = jnp.zeros((quarter, images.shape[1]), jnp.float32)
    for hop_index in range(HOPS):
        if hop_index > 0:
            text_block = from_behind(text_block, "dp", -1)
        logits = SCALE_LOGIT * contract_last(image_unit, text_block) + BIAS_LOGIT
        slopes = (
            SCALE_LOGIT
            * (jax.nn.sigmoid(logits) - (own_mark if hop_index == half_hops else no_mark))
        ).astype(jnp.bfloat16)
        to_image = jnp.dot(slopes, text_block, preferred_element_type=jnp.float32)
        to_text = lax.dot_general(
            slopes, image_unit, (((0,), (0,)), ((), ())), preferred_element_type=jnp.float32
        )
        to_image, to_text = (to_image, to_text)
        grad_image = grad_image + to_image
        if hop_index == 0:
            carried = to_text
        else:
            carried = from_behind(carried, "dp", -1) + to_text
    grad_text_unit = from_behind(carried, "dp", half_hops - 1)
    grad_image_unit = lax.psum(grad_image, "tensor")
    grad_text = (
        grad_text_unit - text_f * jnp.sum(text_f * grad_text_unit, axis=1, keepdims=True)
    ) / text_norm
    output_gradient = (
        grad_image_unit - image_f * jnp.sum(image_f * grad_image_unit, axis=1, keepdims=True)
    ) / image_norm
    grad_out_b = output_gradient.astype(jnp.bfloat16)
    hidden_back, output_back = (
        lax.all_gather(hidden_weight, "dp", axis=0, tiled=True),
        lax.all_gather(output_weight, "dp", axis=1, tiled=True),
    )
    grad_act = contract_last(grad_out_b, output_back)
    pull_back = jax.vjp(gelu_tanh, preact)[1]
    grad_pre = pull_back(grad_act)[0].astype(jnp.bfloat16)
    normed_terms = contract_last(grad_pre, hidden_back)
    normalized_gradient = lax.psum(normed_terms, "tensor")
    standardized_gradient = normalized_gradient * layer_norm_gain
    images_gradient = output_gradient + reciprocal_deviation * (
        standardized_gradient
        - jnp.mean(standardized_gradient, axis=1, keepdims=True)
        - standardized_input
        * jnp.mean(standardized_gradient * standardized_input, axis=1, keepdims=True)
    )
    return (images_gradient, grad_text)


def solution(mesh):
    placed = (P("dp", None), P(), P("dp", "tensor"), P("tensor", "dp"), P(("dp", "tensor"), None))
    return jax.shard_map(
        shards,
        mesh=mesh,
        in_specs=placed,
        out_specs=(P("dp", None), P(("dp", "tensor"), None)),
        check_vma=False,
    )
```

profile of v0, /device:TPU:1, one launch (start us, length us, event | category | flops | bytes accessed | tf_op | source)
XLA Modules:
  0.0 1738.0 jit_solution(4223417832743445676)
XLA Ops:
  8.7 1.0 fusion.99
  9.7 1.2 convert_reduce_fusion
  11.4 617.2 %all-gather.5.cloned.1.call-done = bf16[128,9,1076]{2,1,0:T(8,128)(2,1)} async-done(((bf16[1,9,1076]{2,1,0:T(8,128)(2,1)}), bf16[128,9,1076]{2,1,0:T(8,128)(2,1)}) %all-gather.5.cloned.1.call-update) | async-done | bytes 2479120 | tf_op jit(solution)/shard_map/all_gather | solution.py:47
  628.6 5.9 reshape.41
  634.5 3.0 fusion.76
  637.6 684.9 %all-gather.7.cloned.1.call-done = bf16[128,9,1076]{2,1,0:T(8,128)(2,1)} async-done(((bf16[1,9,1076]{2,1,0:T(8,128)(2,1)}), bf16[128,9,1076]{2,1,0:T(8,128)(2,1)}) %all-gather.7.cloned.1.call-update) | async-done | bytes 2479120 | tf_op jit(solution)/shard_map/all_gather | solution.py:48
  1322.4 6.0 reshape.43
  1328.4 3.9 fusion.88
  1333.3 1.9 collective-permute-start
  1335.3 7.7 collective-permute-done
  1342.9 1.9 collective-permute-start.1
  1344.9 4.5 collective-permute-done.1
  1349.4 7.8 collective-permute-start.2
  1357.2 2.4 collective-permute-done.2
  1359.5 9.8 collective-permute-start.3
  1369.4 2.4 collective-permute-done.3
  1371.7 9.8 collective-permute-start.4
  1381.6 2.4 collective-permute-done.4
  1383.9 9.8 collective-permute-start.5
  1393.8 2.4 collective-permute-done.5
  1396.1 9.8 collective-permute-start.6
  1406.5 1.5 collective-permute-done.6
  1408.1 9.8 collective-permute-start.7
  1417.9 72.7 %all-reduce.4.cloned.1.call-done = f32[256,1152]{1,0:T(8,128)} async-done(((f32[256,1152]{1,0:T(8,128)}), f32[256,1152]{1,0:T(8,128)}) %all-reduce.4.cloned.1.call-update) | async-done | bytes 1179664 | tf_op jit(solution)/shard_map/psum | solution.py:53
  1490.5 1.6 multiply_reduce_fusion.1
  1492.9 8.6 collective-permute-start.8
  1506.7 8.5 collective-permute-start.9
  1515.2 1.4 convolution_add_fusion
  1517.5 1.3 collective-permute-done.9
  1518.9 9.8 collective-permute-start.10
  1529.0 5.5 collective-permute-done.10
  1534.5 9.8 collective-permute-start.11
  1544.6 10.0 collective-permute-done.11
  1554.6 10.1 collective-permute-start.12
  1566.0 8.0 collective-permute-done.12
  1574.7 10.1 collective-permute-start.13
  1584.9 40.9 %all-reduce.6.cloned.1.call-done = f32[256,1152]{1,0:T(8,128)} async-done(((f32[256,1152]{1,0:T(8,128)}), f32[256,1152]{1,0:T(8,128)}) %all-reduce.6.cloned.1.call-update) | async-done | bytes 1179664 | tf_op jit(solution)/shard_map/psum | solution.py:84
  1625.7 2.3 multiply_reduce_fusion
  1628.0 1.8 add.183
  1629.8 6.0 collective-permute-start.14
  1635.8 7.6 fusion.83
  1643.4 1.0 fusion.121
  1644.5 1.0 add.184
  1645.5 1.9 collective-permute-start.15
  1647.4 9.8 collective-permute-done.15
  1658.2 69.8 %all-reduce.8.cloned.1.call-done = f32[256,1152]{1,0:T(8,128)} async-done(((f32[256,1152]{1,0:T(8,128)}), f32[256,1152]{1,0:T(8,128)}) %all-reduce.8.cloned.1.call-update) | async-done | bytes 1179664 | tf_op jit(solution)/shard_map/psum | solution.py:100
  1728.1 1.7 multiply_reduce_fusion.2
  1729.8 1.7 fusion.9
  (93 shorter events, 13.6 us)
Async XLA Ops:
  7.2 3.8 copy-start
  7.2 621.4 %all-gather.5.cloned.1.call-start = ((), (), s32[]{:S(2)}) async-start(), calls=%async_computation.3 | async-start | bytes 4755456 | tf_op jit(solution)/shard_map/all_gather | solution.py:47
  7.9 1314.5 %all-gather.7.cloned.1.call-start = ((), (), s32[]{:S(2)}) async-start(), calls=%async_computation.4 | async-start | bytes 4755456 | tf_op jit(solution)/shard_map/all_gather | solution.py:48
  8.7 1481.9 %all-reduce.4.cloned.1.call-start = ((), (), s32[]{:S(2)}) async-start(), calls=%async_computation | async-start | bytes 2359296 | tf_op jit(solution)/shard_map/psum | solution.py:53
  11.3 1321.1 %copy-start.16 = (f32[64]{0:T(128)}, f32[64]{0:T(128)S(1)}, u32[]{:S(2)}) copy-start(f32[64]{0:T(128)S(1)} %add_sqrt_fusion.1) | copy-start | bytes 772
  11.3 623.2 %copy-start.14 = (f32[256]{0:T(256)}, f32[256]{0:T(256)S(1)}, u32[]{:S(2)}) copy-start(f32[256]{0:T(256)S(1)} %add_rsqrt_fusion) | copy-start | bytes 3076
  11.3 623.2 %copy-start.13 = (f32[1152]{0:T(1024)S(1)}, f32[1152]{0:T(1024)}, u32[]{:S(2)}) copy-start(f32[1152]{0:T(1024)} %param.6) | copy-start | bytes 13828
  637.5 690.8 %copy-start.20 = (f32[256,1076]{0,1:T(8,128)}, f32[256,1076]{0,1:T(8,128)S(1)}, u32[]{:S(2)}) copy-start(f32[256,1076]{0,1:T(8,128)S(1)} %fusion.76) | copy-start | bytes 3305476
  1332.3 0.9 copy-start.4
  1332.4 293.4 %all-reduce.6.cloned.1.call-start = ((), (), s32[]{:S(2)}) async-start(), calls=%async_computation.1 | async-start | bytes 2359296 | tf_op jit(solution)/shard_map/psum | solution.py:84
  1333.3 9.6 collective-permute-start
  1342.9 6.5 collective-permute-start.1
  1349.4 10.1 collective-permute-start.2
  1359.5 12.2 collective-permute-start.3
  1371.7 12.2 collective-permute-start.4
  1383.9 12.2 collective-permute-start.5
  1396.1 11.9 collective-permute-start.6
  1408.1 97.7 %collective-permute-start.7 = (bf16[64,1152]{1,0:T(8,128)(2,1)S(1)}, bf16[64,1152]{1,0:T(8,128)(2,1)S(1)}, u32[]{:S(2)}, u32[]{:S(2)}) collective-permute-start(bf16[64,1152]{1,0:T(8,128)(2,1)S(1)} %collective-permute-done.6), channel_id=1, source_target_pairs={{0,508},{4,0},{8,4},{12,8},{16,12},{20,16},{24,20},{28,24},{32,28}... | collective-permute-start | bytes 442376 | tf_op jit(solution)/shard_map/ppermute | solution.py:16
  1490.5 1.6 copy-start.1
  1492.9 13.5 collective-permute-start.8
  1502.2 1.8 copy-start.11
  1502.5 1.8 copy-start.9
  1502.5 0.7 copy-start.19
  1502.9 2.1 copy-start.7
  1506.1 9.1 copy-start.6
  1506.7 12.2 collective-permute-start.9
  1516.6 0.8 copy-start.12
  1516.6 12.1 copy-start.10
  1516.6 211.4 %all-reduce.8.cloned.1.call-start = ((), (), s32[]{:S(2)}) async-start(), calls=%async_computation.2 | async-start | bytes 2359296 | tf_op jit(solution)/shard_map/psum | solution.py:100
  1518.9 15.6 collective-permute-start.10
  1528.9 35.8 %copy-start.8 = (bf16[256,64]{0,1:T(8,128)(2,1)S(1)}, bf16[256,64]{0,1:T(8,128)(2,1)}, u32[]{:S(2)}) copy-start(bf16[256,64]{0,1:T(8,128)(2,1)} %copy-done.7) | copy-start | bytes 98308
  1534.5 20.1 %collective-permute-start.11 = (f32[64,1152]{1,0:T(8,128)S(1)}, f32[64,1152]{1,0:T(8,128)S(1)}, u32[]{:S(2)}, u32[]{:S(2)}) collective-permute-start(f32[64,1152]{1,0:T(8,128)S(1)} %add.180), channel_id=1, source_target_pairs={{0,508},{4,0},{8,4},{12,8},{16,12},{20,16},{24,20},{28,24},{32,28}... | collective-permute-start | bytes 884744 | tf_op jit(solution)/shard_map/ppermute | solution.py:16
  1554.6 19.4 %collective-permute-start.12 = (f32[64,1152]{1,0:T(8,128)S(1)}, f32[64,1152]{1,0:T(8,128)S(1)}, u32[]{:S(2)}, u32[]{:S(2)}) collective-permute-start(f32[64,1152]{1,0:T(8,128)S(1)} %add.181), channel_id=1, source_target_pairs={{0,508},{4,0},{8,4},{12,8},{16,12},{20,16},{24,20},{28,24},{32,28}... | collective-permute-start | bytes 884744 | tf_op jit(solution)/shard_map/ppermute | solution.py:16
  1574.7 53.3 %collective-permute-start.13 = (f32[64,1152]{1,0:T(8,128)}, f32[64,1152]{1,0:T(8,128)}, u32[]{:S(2)}, u32[]{:S(2)}) collective-permute-start(f32[64,1152]{1,0:T(8,128)} %add.182), channel_id=1, source_target_pairs={{0,508},{4,0},{8,4},{12,8},{16,12},{20,16},{24,20},{28,24},{32,28}... | collective-permute-start | bytes 884744 | tf_op jit(solution)/shard_map/ppermute | solution.py:16
  1625.7 10.1 copy-start.2
  1629.8 14.7 collective-permute-start.14
  1643.4 13.7 copy-start.5
  1643.4 13.7 copy-start.17
  1644.5 83.6 %copy-start.15 = (f32[256]{0:T(256)S(1)}, f32[256]{0:T(256)}, u32[]{:S(2)}) copy-start(f32[256]{0:T(256)} %copy-done.14) | copy-start | bytes 3076
  1645.5 11.7 collective-permute-start.15
  1657.4 72.4 %copy-start.18 = (f32[256]{0:T(256)S(1)}, f32[256]{0:T(256)}, u32[]{:S(2)}) copy-start(f32[256]{0:T(256)} %multiply_reduce_fusion) | copy-start | bytes 3076
  1728.1 1.8 copy-start.3
Sparse Core Ops, SparseCore 0:
  10.1 618.4 all-gather.4
  630.7 691.7 all-gather.6
  1332.5 158.0 all-reduce.3
  1516.7 108.9 all-reduce.5
  1643.5 84.4 all-reduce.7
where the time goes:
time: 1740 us
  waiting for transfers between devices  1540 us (89%)
  starting transfers between devices  126 us (7%)
  matrix products  24.3 us (1%)
    all_gather x1, waiting for transfers between devices, shards(): lax.all_gather(output_weight, 'dp', axis=1, tiled=True)  685 us
    all_gather x1, waiting for transfers between devices, shards(): lax.all_gather(hidden_weight, 'dp', axis=0, tiled=True)  617 us
    ppermute x16, starting transfers between devices, from_behind(): lax.ppermute(array, axis, [(i, (i + by) % peers) for i in range(peers)])  126 us
    psum x1, waiting for transfers between devices, shards(): head_out = features + lax.psum(head_terms, 'tensor')  72.7 us
    psum x1, waiting for transfers between devices, shards(): normalized_gradient = lax.psum(normed_terms, 'tensor')  69.8 us
    ppermute x16, waiting for transfers between devices, from_behind(): lax.ppermute(array, axis, [(i, (i + by) % peers) for i in range(peers)])  57.9 us
    psum x1, waiting for transfers between devices, shards(): grad_image_unit = lax.psum(grad_image, 'tensor')  40.9 us
  transfers between devices with their start and end apart: 21, of which 17 were waited for; matrix products, arithmetic and copies ran while one was open for 2% of the time, Pallas kernels for 0%

commit v1 on v0

v1 whole, which is shorter than its diff:
```python
import jax
import jax.numpy as jnp
import numpy as np
from jax import lax
from jax.experimental import pallas as pl
from jax.experimental.pallas import tpu as pltpu
from jax.sharding import PartitionSpec as P

SCALE_LOGIT = 10.0
BIAS_LOGIT = -3.0
EPS = 1e-06

NX, NZ, NY, NLO = 4, 8, 8, 4
D = 1152
FW = 1152
OWN = 9
MESH = pl.DeviceIdType.MESH
BF = jnp.bfloat16
F32 = jnp.float32
GELU_C = 0.7978845608028654
GELU_A = 0.044715


def contract_last(left, right):
    return lax.dot_general(left, right, (((1,), (1,)), ((), ())), preferred_element_type=F32)


def ident(x, z, y, c):
    return (x * (NZ * NLO) + z * NLO + lax.rem(y, NLO), (y // NLO) * 2 + c)


class Ring:
    def __init__(self, buf, size, pos, after, before, chunks, half, ssem, rsem):
        self.buf, self.size, self.pos = buf, size, pos
        self.rows = buf.shape[0] // size
        self.peer = (after, before)
        self.chunks, self.half = chunks, half
        self.ssem, self.rsem = ssem, rsem
        self.steps = size // 2

    def own(self):
        return pl.ds(pl.multiple_of(self.pos * self.rows, 16), self.rows)

    def kept(self, step, way):
        ids = list(range(len(self.chunks)))
        if step < self.steps:
            return ids
        return ids[: self.half] if way == 0 else ids[self.half :]

    def copy(self, step, way, ch, back):
        move = back if way == 0 else -back
        slot = lax.rem(self.pos - move + 2 * self.size, self.size)
        off, rows = self.chunks[ch]
        ref = self.buf.at[pl.ds(pl.multiple_of(slot * self.rows + off, 16), rows)]
        return pltpu.make_async_remote_copy(
            src_ref=ref,
            dst_ref=ref,
            send_sem=self.ssem.at[step - 1, way, ch],
            recv_sem=self.rsem.at[step - 1, way, ch],
            device_id=self.peer[way],
            device_id_type=MESH,
        )

    def each(self, step):
        for ch in range(len(self.chunks)):
            for way in (0, 1):
                if ch in self.kept(step, way):
                    yield way, ch

    def start(self):
        for way, ch in self.each(1):
            self.copy(1, way, ch, 0).start()

    def forward(self, step):
        for way, ch in self.each(step):
            self.copy(step, way, ch, step).wait_recv()
            if step < self.steps and ch in self.kept(step + 1, way):
                self.copy(step + 1, way, ch, step).start()

    def finish(self):
        for step in range(1, self.steps + 1):
            for way, ch in self.each(step):
                self.copy(step, way, ch, step - 1).wait_send()


CH48 = ((0, 32), (32, 16))
CH144 = ((0, 48), (48, 32), (80, 32), (112, 32))
CH288 = ((0, 80), (80, 64), (144, 80), (224, 64))


def pack_matrix(groups, rows_in, rows_out, used):
    shape = (rows_out, groups * rows_in)
    row = lax.broadcasted_iota(jnp.int32, shape, 0)
    col = lax.broadcasted_iota(jnp.int32, shape, 1)
    hit = jnp.zeros(shape, F32)
    for g in range(groups):
        inner = col - g * rows_in
        hit = jnp.where((inner >= 0) & (inner < used) & (row == inner + g * used), 1.0, hit)
    return hit.astype(BF)


def column_loop(body):
    @pl.loop(0, 3)
    def _(k):
        body(pl.ds(pl.multiple_of(k * 384, 128), 384))


def ln_stats(v):
    v = v - jnp.sum(v, axis=1, keepdims=True) * (1.0 / D)
    var = jnp.sum(v * v, axis=1, keepdims=True) * (1.0 / D)
    rdev = 1.0 / jnp.sqrt(var + EPS)
    return v * rdev, rdev


def kernel(
    images, gain, h_own, o_own, text, order,
    out_img, out_text,
    hy, oy, hx, hz, oz, ox, xin, perm, npm, act, preact, dgel, part,
    cs, cr, es, er, unit, head, inorm, gout, gob, gpre, texts, tunit, tgs, tgr, slopes, slopes_t, accb, gnat,
    y_ss, y_rs, im_ss, im_rs, hx_ss, hx_rs, hz_ss, hz_rs, oz_ss, oz_rs, ox_ss, ox_rs,
    tx_ss, tx_rs, tg_ss, tg_rs, sw_ss, sw_rs,
):
    a = lax.axis_index("dp")
    t = lax.axis_index("tensor")
    x, z, lo = a // (NZ * NLO), lax.rem(a // NLO, NZ), lax.rem(a, NLO)
    h, c = t // 2, lax.rem(t, 2)
    y = h * NLO + lo
    p = lax.rem(lo, 2)
    q = p * 2 + c
    a0 = a - p
    n_dp = NX * NZ * NLO
    mine = p == h

    core = ident(x, z, y, 1 - c)
    pair = ident(x, z, y + 1 - 2 * p, c)
    far = ident(x, z, lax.rem(y + NLO, NY), c)
    x_up = ident(lax.rem(x + 1, NX), z, y, c)
    x_dn = ident(lax.rem(x + NX - 1, NX), z, y, c)
    z_up = ident(x, lax.rem(z + 1, NZ), y, c)
    z_dn = ident(x, lax.rem(z + NZ - 1, NZ), y, c)

    def owner(j):
        return (lax.rem(a0 - 4 + j + n_dp, n_dp), q)

    def user(i, half):
        return (lax.rem(a - p - 4 + 2 * i + h + n_dp, n_dp), half * 2 + c)

    def each_owner(body):
        for j in range(9):

            @pl.when(jnp.logical_not(mine & (p + 4 == j)))
            def _():
                body(j)

    def each_user(body):
        for i in range(5):
            for half in range(2):
                here = jnp.logical_not(mine & (h == half)) if i == 2 else None
                if i == 0:
                    here = p == 0
                if here is None:
                    body(i, half)
                else:

                    @pl.when(here)
                    def _():
                        body(i, half)

    def remote(src, dst, ss, rs, device):
        return pltpu.make_async_remote_copy(
            src_ref=src, dst_ref=dst, send_sem=ss, recv_sem=rs, device_id=device, device_id_type=MESH
        )

    def slab(k, rows):
        return pl.ds(k * rows if isinstance(k, int) else pl.multiple_of(k * rows, rows), rows)

    bar = pltpu.get_barrier_semaphore()

    def signal(device):
        pl.semaphore_signal(bar, inc=1, device_id=device, device_id_type=MESH)

    for device in (core, pair, far, x_up, x_dn, z_up, z_dn):
        signal(device)
    for l in range(NLO):

        @pl.when(jnp.logical_not((4 * p + l) == y))
        def _():
            signal(ident(x, z, 4 * p + l, c))

    each_owner(lambda j: signal(owner(j)))
    each_user(lambda i, half: signal(user(i, half)))
    pl.semaphore_wait(bar, 30 - 3 * mine.astype(jnp.int32) - 2 * p)

    for which, (src, dst) in enumerate(((h_own, hy), (o_own, oy))):
        for i in range(4):

            @pl.when(jnp.logical_not((h + 2 * i) == y))
            def _():
                remote(
                    src, dst.at[slab(lo, 16)], y_ss.at[which, i], y_rs.at[which, lo], ident(x, z, h + 2 * i, c)
                ).start()

            @pl.when((h + 2 * i) == y)
            def _():
                dst[slab(lo, 16), :] = src[...]

    def im_copy(k, block):
        return remote(
            images.at[slab(2 * h + k, 64)], xin.at[slab(2 * k + block, 64)], im_ss.at[k], im_rs.at[k], pair
        )

    for k in range(2):
        im_copy(k, p).start()
        xin[slab(2 * k + p, 64), :] = images[slab(2 * h + k, 64), :]

    tx = text[...].astype(F32)
    text_norm = jnp.sqrt(jnp.sum(tx * tx, axis=1, keepdims=True) + EPS)
    tunit[...] = (tx / text_norm).astype(BF)

    def tx_copy(i, half):
        j = p + 8 - 2 * i
        return remote(tunit, texts.at[slab(j, 64)], tx_ss.at[i, half], tx_rs.at[j], user(i, half))

    each_user(lambda i, half: tx_copy(i, half).start())
    texts[slab(9, 64), :] = jnp.zeros((64, D), BF)

    @pl.when(mine)
    def _():
        texts[slab(p + 4, 64), :] = tunit[...]

    @pl.when(p == 1)
    def _():
        tgr[pl.ds(0, 128), :] = jnp.zeros((128, D), BF)

    ring_hx = Ring(hx, NX, x, x_up, x_dn, CH48, 1, hx_ss, hx_rs)
    ring_hz = Ring(hz, NZ, z, z_up, z_dn, CH144, 2, hz_ss, hz_rs)
    ring_oz = Ring(oz, NZ, z, z_up, z_dn, CH48, 1, oz_ss, oz_rs)
    ring_ox = Ring(ox, NX, x, x_up, x_dn, CH288, 2, ox_ss, ox_rs)

    pack_y = pack_matrix(NLO, 16, 48, OWN)

    def y_wait(which, src, dst):
        for l in range(NLO):

            @pl.when(jnp.logical_not((4 * p + l) == y))
            def _():
                remote(src, dst.at[slab(l, 16)], y_ss.at[which, 0], y_rs.at[which, l], pair).wait_recv()

    y_wait(0, h_own, hy)
    hx[ring_hx.own(), :] = jnp.dot(pack_y, hy[...], preferred_element_type=F32).astype(BF)
    ring_hx.start()
    y_wait(1, o_own, oy)
    oz[ring_oz.own(), :] = jnp.dot(pack_y, oy[...], preferred_element_type=F32).astype(BF)
    ring_oz.start()
    ring_hx.forward(1)
    ring_oz.forward(1)
    ring_hx.forward(2)
    pack_x = pack_matrix(NX, 48, 144, 4 * OWN)
    hz[ring_hz.own(), :] = jnp.dot(pack_x, hx[...], preferred_element_type=F32).astype(BF)
    ring_oz.forward(2)
    ring_hz.start()
    ring_oz.forward(3)

    @pl.loop(0, 9)
    def _(k):
        rows = lax.broadcasted_iota(jnp.int32, (128, D), 0) + k * 128
        perm[slab(k, 128), :] = jnp.where(rows == order[...], 1.0, 0.0).astype(BF)

    for k in range(2):
        im_copy(k, 1 - p).wait_recv()

    @pl.loop(0, 4)
    def _(r):
        xhat, _ = ln_stats(xin[slab(r, 64), :].astype(F32))
        unit[slab(r, 64), :] = (xhat * gain[...]).astype(BF)

    def permute_normed(cols):
        npm[:, cols] = jnp.dot(unit[...], perm[:, cols], preferred_element_type=F32).astype(BF)

    column_loop(permute_normed)

    ring_oz.forward(4)

    def pack_ox(cols):
        pack_z = pack_matrix(NZ, 48, 288, 4 * OWN)
        ox[ring_ox.own(), cols] = jnp.dot(pack_z, oz[:, cols], preferred_element_type=F32).astype(BF)

    column_loop(pack_ox)
    ring_ox.start()
    ring_hz.forward(1)
    ring_hz.forward(2)
    ring_ox.forward(1)
    ring_hz.forward(3)
    ring_hz.forward(4)

    def hidden(cols):
        v = jnp.dot(npm[...], hz[:, cols], preferred_element_type=F32)
        preact[:, cols] = v
        act[:, cols] = (0.5 * v * (1.0 + jnp.tanh(GELU_C * (v + GELU_A * (v * v * v))))).astype(BF)

    column_loop(hidden)
    ring_ox.forward(2)

    def head_terms(cols):
        part[:, cols] = contract_last(act[...], ox[cols, :])

    column_loop(head_terms)

    own_rows = slab(c, 128)
    other_rows = slab(1 - c, 128)

    def swap(n, src, dst, device):
        return remote(src, dst, sw_ss.at[n], sw_rs.at[n], device)

    def core_sum(n, k):
        cs[slab(k, 128), :] = part[other_rows, :].astype(BF)
        move = swap(n, cs.at[slab(k, 128)], cr.at[slab(k, 128)], core)
        move.start()
        move.wait_recv()
        accb[...] = part[own_rows, :] + cr[slab(k, 128), :].astype(F32)
        return move

    moves = [core_sum(0, 0)]
    es[slab(0, 128), :] = accb[...].astype(BF)
    moves.append(swap(1, es.at[slab(0, 128)], er.at[slab(0, 128)], pair))
    moves[-1].start()

    def gelu_slope(cols):
        v = preact[:, cols]
        th = jnp.tanh(GELU_C * (v + GELU_A * (v * v * v)))
        inner = GELU_C * (1.0 + (3.0 * GELU_A) * (v * v))
        dgel[:, cols] = 0.5 * (1.0 + th) + 0.5 * v * (1.0 - th * th) * inner

    column_loop(gelu_slope)
    moves[-1].wait_recv()

    @pl.loop(0, 2)
    def _(b):
        rows = slab(b, 64)
        out = xin[slab(2 * c + b, 64), :].astype(F32) + accb[rows, :] + er[rows, :].astype(F32)
        norm = jnp.sqrt(jnp.sum(out * out, axis=1, keepdims=True) + EPS)
        out = out / norm
        head[rows, :] = out
        inorm[rows, :] = jnp.broadcast_to(norm, (64, 128))
        unit[slab(2 * c + b, 64), :] = out.astype(BF)

    moves.append(swap(2, unit.at[own_rows], unit.at[own_rows], core))
    moves[-1].start()
    each_owner(lambda j: remote(tunit, texts.at[slab(j, 64)], tx_ss.at[0, 0], tx_rs.at[j], pair).wait_recv())
    swap(2, unit.at[other_rows], unit.at[other_rows], core).wait_recv()

    own_quarter = 2 * h

    def slope(dots, row, col):
        block = lax.shift_right_logical(row, 6) & 1
        scored = (col >= block * 64) & (col < 512 + block * 64)
        match = (col == 256 + block * 64 + (row & 63)) & (lax.shift_right_logical(row, 7) + own_quarter == q)
        value = jax.nn.sigmoid(SCALE_LOGIT * dots + BIAS_LOGIT) - jnp.where(match, 1.0, 0.0)
        return jnp.where(scored, SCALE_LOGIT * value, 0.0).astype(BF)

    @pl.loop(0, 5)
    def _(k):
        cols = slab(k, 128)
        row = lax.broadcasted_iota(jnp.int32, (256, 128), 0)
        col = lax.broadcasted_iota(jnp.int32, (256, 128), 1) + k * 128
        slopes[:, cols] = slope(contract_last(unit[...], texts[cols, :]), row, col)

    def to_image(cols):
        part[:, cols] = jnp.dot(slopes[...], texts[:, cols], preferred_element_type=F32)

    column_loop(to_image)
    moves.append(core_sum(3, 1))
    es[slab(1, 128), :] = accb[...].astype(BF)
    moves.append(swap(4, es.at[slab(1, 128)], er.at[slab(1, 128)], pair))
    moves[-1].start()

    @pl.loop(0, 5)
    def _(k):
        rows = slab(k, 128)
        row = lax.broadcasted_iota(jnp.int32, (128, 256), 1)
        col = lax.broadcasted_iota(jnp.int32, (128, 256), 0) + k * 128
        slopes_t[rows, :] = slope(contract_last(texts[rows, :], unit[...]), row, col)

    def to_text(cols):
        tgs[:, cols] = jnp.dot(slopes_t[...], unit[:, cols], preferred_element_type=F32).astype(BF)

    column_loop(to_text)

    moves[-1].wait_recv()

    @pl.loop(0, 2)
    def _(b):
        rows = slab(b, 64)
        g = accb[rows, :] + er[pl.ds(pl.multiple_of(128 + b * 64, 64), 64), :].astype(F32)
        f = head[rows, :]
        out = (g - f * jnp.sum(f * g, axis=1, keepdims=True)) / inorm[rows, 0:1]
        gout[rows, :] = out
        gob[slab(2 * c + b, 64), :] = out.astype(BF)

    moves.append(swap(5, gob.at[own_rows], gob.at[own_rows], core))
    moves[-1].start()

    def tg_copy(j):
        i = (j % 2 + 8 - j) // 2
        return remote(
            tgs.at[slab(j, 64)], tgr.at[slab(2 * i + h, 64)], tg_ss.at[j], tg_rs.at[2 * i + h], owner(j)
        )

    each_owner(lambda j: tg_copy(j).start())

    @pl.when(mine)
    def _():
        tgr[slab(4 + h, 64), :] = tgs[slab(4 + p, 64), :]

    swap(5, gob.at[other_rows], gob.at[other_rows], core).wait_recv()

    def hidden_back(cols):
        g = jnp.dot(gob[...], ox[:, cols], preferred_element_type=F32)
        gpre[:, cols] = (g * dgel[:, cols]).astype(BF)

    column_loop(hidden_back)

    def normed_terms(cols):
        part[:, cols] = contract_last(gpre[...], hz[cols, :])

    column_loop(normed_terms)
    moves.append(core_sum(6, 2))
    es[pl.ds(256, 64), :] = accb[slab(1 - p, 64), :].astype(BF)
    moves.append(swap(7, es.at[pl.ds(256, 64)], er.at[pl.ds(256, 64)], pair))
    moves[-1].start()
    xhat, rdev = ln_stats(xin[slab(2 * c + p, 64), :].astype(F32))
    moves[-1].wait_recv()
    total = accb[slab(p, 64), :] + er[pl.ds(256, 64), :].astype(F32)
    high = total.astype(BF)
    low = (total - high.astype(F32)).astype(BF)

    @pl.loop(0, 3)
    def _(k):
        cols = pl.ds(pl.multiple_of(k * 384, 128), 384)
        gnat[:, cols] = contract_last(high, perm[cols, :]) + contract_last(low, perm[cols, :])

    g = gnat[...] * gain[...]
    mean_g = jnp.sum(g, axis=1, keepdims=True) * (1.0 / D)
    mean_gx = jnp.sum(g * xhat, axis=1, keepdims=True) * (1.0 / D)
    done = slab(2 * h + c, 64)
    out_img[done, :] = (gout[slab(p, 64), :] + rdev * (g - mean_g - xhat * mean_gx)).astype(BF)
    for n, device in ((8, far), (9, core)):
        moves.append(swap(n, out_img.at[done], out_img.at[done], device))
        moves[-1].start()

    each_user(lambda i, half: remote(
        tunit, tgr.at[slab(2 * i + half, 64)], tg_ss.at[0], tg_rs.at[2 * i + half], pair
    ).wait_recv())
    g = tgr[pl.ds(0, 64), :].astype(F32)
    for k in range(1, 10):
        g = g + tgr[slab(k, 64), :].astype(F32)
    tx = text[...].astype(F32)
    text_norm = jnp.sqrt(jnp.sum(tx * tx, axis=1, keepdims=True) + EPS)
    text_f = tx / text_norm
    out_text[...] = (g - text_f * jnp.sum(text_f * g, axis=1, keepdims=True)) / text_norm

    from_far = slab(2 * (1 - h) + c, 64)
    swap(8, out_img.at[from_far], out_img.at[from_far], far).wait_recv()
    moves.append(swap(10, out_img.at[from_far], out_img.at[from_far], core))
    moves[-1].start()
    from_core = slab(2 * h + 1 - c, 64)
    swap(9, out_img.at[from_core], out_img.at[from_core], core).wait_recv()
    from_both = slab(2 * (1 - h) + 1 - c, 64)
    swap(10, out_img.at[from_both], out_img.at[from_both], core).wait_recv()

    for which, (src, dst) in enumerate(((h_own, hy), (o_own, oy))):
        for i in range(4):

            @pl.when(jnp.logical_not((h + 2 * i) == y))
            def _():
                remote(
                    src, dst.at[slab(lo, 16)], y_ss.at[which, i], y_rs.at[which, lo], ident(x, z, h + 2 * i, c)
                ).wait_send()

    for k in range(2):
        im_copy(k, p).wait_send()
    each_user(lambda i, half: tx_copy(i, half).wait_send())
    each_owner(lambda j: tg_copy(j).wait_send())
    for ring in (ring_hx, ring_hz, ring_oz, ring_ox):
        ring.finish()
    for move in moves:
        move.wait_send()


def feature_order():
    z, x, j = np.meshgrid(np.arange(NZ), np.arange(NX), np.arange(NLO * OWN), indexing="ij")
    return (x * (NZ * NLO * OWN) + z * (NLO * OWN) + j).reshape(1, D).astype(np.int32)


def shards(images, layer_norm_gain, hidden_weight, output_weight, text):
    width = hidden_weight.shape[1]
    pad = ((0, 16 - OWN), (0, FW - width))
    h_own = jnp.pad(hidden_weight, pad)
    o_own = jnp.pad(output_weight.T, pad)

    def vm(rows, cols, kind=BF):
        return pltpu.VMEM((rows, cols), kind)

    dma = pltpu.SemaphoreType.DMA
    scratch = [
        vm(64, FW), vm(64, FW), vm(192, FW), vm(D, FW), vm(384, FW), vm(D, FW),
        vm(256, D), vm(D, D), vm(256, D), vm(256, FW), vm(256, FW, F32), vm(256, FW, F32), vm(256, D, F32),
        vm(384, D), vm(384, D), vm(320, D), vm(320, D),
        vm(256, D), vm(128, D, F32), vm(128, 128, F32), vm(128, D, F32), vm(256, D), vm(256, FW),
        vm(640, D), vm(64, D), vm(640, D), vm(640, D), vm(256, 640), vm(640, 256), vm(128, D, F32), vm(64, D, F32),
        dma((2, 4)), dma((2, 4)), dma((2,)), dma((2,)),
        dma((2, 2, 2)), dma((2, 2, 2)), dma((4, 2, 4)), dma((4, 2, 4)),
        dma((4, 2, 2)), dma((4, 2, 2)), dma((2, 2, 4)), dma((2, 2, 4)),
        dma((5, 2)), dma((9,)), dma((9,)), dma((10,)), dma((11,)), dma((11,)),
    ]
    vmem = pl.BlockSpec(memory_space=pltpu.VMEM)
    images_gradient, grad_text = pl.pallas_call(
        kernel,
        out_shape=(jax.ShapeDtypeStruct((256, D), BF), jax.ShapeDtypeStruct((64, D), F32)),
        in_specs=[vmem] * 6,
        out_specs=(vmem, vmem),
        scratch_shapes=scratch,
        compiler_params=pltpu.CompilerParams(
            collective_id=0, has_side_effects=True, vmem_limit_bytes=56 * 2**20
        ),
        cost_estimate=pl.CostEstimate(flops=4 * 10**9, bytes_accessed=4 * 10**6, transcendentals=10**6),
    )(images, layer_norm_gain.reshape(1, D), h_own, o_own, text, jnp.asarray(feature_order()))
    return images_gradient.astype(F32), grad_text


def solution(mesh):
    placed = (P("dp", None), P(), P("dp", "tensor"), P("tensor", "dp"), P(("dp", "tensor"), None))
    return jax.shard_map(
        shards,
        mesh=mesh,
        in_specs=placed,
        out_specs=(P("dp", None), P(("dp", "tensor"), None)),
        check_vma=False,
    )
```

time: 1740 us -> 174 us (0.10)
  the two profiles are of different devices: /device:TPU:1 before, /device:TPU:25 now
where the time goes in v1:
time: 174 us
  Pallas kernels  166 us (95%)
  local copies, waits for them, and re-layouts  4.79 us (3%)
  other arithmetic  2.2 us (1%)
    pallas_call x1, Pallas kernels, shards(): pl.pallas_call(kernel, out_shape=(jax.ShapeDtypeStruct((256, D), BF), jax...  166 us

profile of v1, /device:TPU:25, one launch (start us, length us, event | category | flops | bytes accessed | tf_op | source)
XLA Modules:
  0.0 173.6 jit_solution(15680488868592992868)
XLA Ops:
  0.6 1.3 reshape.7.gain
  1.9 1.4 pad.7.h_own
  3.3 1.4 pad.8.o_own
  4.7 165.9 %shard_map.77 = (bf16[256,1152]{1,0:T(8,128)(2,1)}, f32[64,1152]{1,0:T(8,128)}) custom-call(bf16[256,1152]{1,0:T(8,128)(2,1)} %images.1, f32[1,1152]{1,0:T(1,128)} %reshape.7.gain, bf16[16,1152]{1,0:T(8,128)(2,1)} %pad.7.h_own, bf16[16,1152]{1,0:T(8,128)(2,1)} %pad.8.o_own, bf16[64,1152]{1,0:T(8,128)(2,1)} %text.1, s32[1,1152]{1,0:T(1,128)} %constant.5.clone.order), custom_call_target="tpu_custom_call" | custom-call | flops 4000000000 | bytes 4000000 | tf_op jit(solution)/shard_map/pallas_call | solution.py:517
  170.7 0.0 copy-start
  170.7 2.2 %convert_element_type.6 = f32[256,1152]{1,0:T(8,128)} convert(bf16[256,1152]{1,0:T(8,128)(2,1)} %get-tuple-element.4) | non-fusion elementwise | flops 294912 | bytes 1769472 | tf_op jit(solution)/shard_map/convert_element_type | solution.py:528
  172.9 0.0 copy-done
  172.9 0.7 copy.9
Async XLA Ops:
  170.7 2.2 %copy-start = (f32[64,1152]{1,0:T(8,128)S(1)}, f32[64,1152]{1,0:T(8,128)}, u32[]{:S(2)}) copy-start(f32[64,1152]{1,0:T(8,128)} %get-tuple-element.9) | copy-start | bytes 884740

commit v2 on v1

v2 whole, which is shorter than its diff:
```python
import jax
import jax.numpy as jnp
import numpy as np
from jax import lax
from jax.experimental import pallas as pl
from jax.experimental.pallas import tpu as pltpu
from jax.sharding import PartitionSpec as P

SCALE_LOGIT = 10.0
BIAS_LOGIT = -3.0
EPS = 1e-06

NX, NZ, NY, NLO = 4, 8, 8, 4
D = 1152
FW = 1152
OWN = 9
MESH = pl.DeviceIdType.MESH
BF = jnp.bfloat16
F32 = jnp.float32
GELU_C = 0.7978845608028654
GELU_A = 0.044715


def contract_last(left, right):
    return lax.dot_general(left, right, (((1,), (1,)), ((), ())), preferred_element_type=F32)


def ident(x, z, y, c):
    return (x * (NZ * NLO) + z * NLO + lax.rem(y, NLO), (y // NLO) * 2 + c)


class Net:
    def __init__(self):
        self.sends, self.arrivals = [], {}

    def start(self, copy, name, arrival=None):
        copy.start()
        self.sends.append(copy.wait_send)
        self.arrivals[name] = (arrival or copy).wait_recv

    def wait(self, name):
        self.arrivals.pop(name)()

    def drain(self):
        for name in list(self.arrivals):
            self.wait(name)
        for wait_send in self.sends:
            wait_send()


class Ring:
    def __init__(self, net, buf, size, pos, after, before, chunks, half, ssem, rsem):
        self.net, self.buf, self.size, self.pos = net, buf, size, pos
        self.rows = buf.shape[0] // size
        self.peer = (after, before)
        self.chunks, self.half = chunks, half
        self.ssem, self.rsem = ssem, rsem
        self.steps = size // 2

    def own(self):
        return pl.ds(pl.multiple_of(self.pos * self.rows, 16), self.rows)

    def kept(self, step, way):
        ids = list(range(len(self.chunks)))
        if step < self.steps:
            return ids
        return ids[: self.half] if way == 0 else ids[self.half :]

    def copy(self, step, way, ch, back):
        move = back if way == 0 else -back
        slot = lax.rem(self.pos - move + 2 * self.size, self.size)
        off, rows = self.chunks[ch]
        ref = self.buf.at[pl.ds(pl.multiple_of(slot * self.rows + off, 16), rows)]
        return pltpu.make_async_remote_copy(
            src_ref=ref,
            dst_ref=ref,
            send_sem=self.ssem.at[step - 1, way, ch],
            recv_sem=self.rsem.at[step - 1, way, ch],
            device_id=self.peer[way],
            device_id_type=MESH,
        )

    def each(self, step):
        for ch in range(len(self.chunks)):
            for way in (0, 1):
                if ch in self.kept(step, way):
                    yield way, ch

    def send(self, step, way, ch):
        sent, comes = self.copy(step, way, ch, step - 1), self.copy(step, way, ch, step)
        self.net.start(sent, (self, step, way, ch), comes)

    def start(self):
        for way, ch in self.each(1):
            self.send(1, way, ch)

    def forward(self, step):
        for way, ch in self.each(step):
            self.net.wait((self, step, way, ch))
            if step < self.steps and ch in self.kept(step + 1, way):
                self.send(step + 1, way, ch)


CH48 = ((0, 32), (32, 16))
CH144 = ((0, 48), (48, 32), (80, 32), (112, 32))
CH288 = ((0, 80), (80, 64), (144, 80), (224, 64))


def pack_matrix(groups, rows_in, rows_out, used):
    shape = (rows_out, groups * rows_in)
    row = lax.broadcasted_iota(jnp.int32, shape, 0)
    col = lax.broadcasted_iota(jnp.int32, shape, 1)
    hit = jnp.zeros(shape, F32)
    for g in range(groups):
        inner = col - g * rows_in
        hit = jnp.where((inner >= 0) & (inner < used) & (row == inner + g * used), 1.0, hit)
    return hit.astype(BF)


def column_loop(body):
    @pl.loop(0, 3)
    def _(k):
        body(pl.ds(pl.multiple_of(k * 384, 128), 384))


def ln_stats(v):
    v = v - jnp.sum(v, axis=1, keepdims=True) * (1.0 / D)
    var = jnp.sum(v * v, axis=1, keepdims=True) * (1.0 / D)
    rdev = 1.0 / jnp.sqrt(var + EPS)
    return v * rdev, rdev


def stages(
    net, images, gain_in, h_in, o_in, text, order,
    out_img, out_text,
    h_own, o_own, hy, oy, hx, hz, oz, ox, xin, perm, npm, act, preact, dgel, part,
    cs, cr, es, er, unit, head, inorm, gout, gob, gpre, texts, tz, tgs, from_next, from_last, tgy, tgr, slopes, slopes_t, accb, gnat,
    y_ss, y_rs, im_ss, im_rs, hx_ss, hx_rs, hz_ss, hz_rs, oz_ss, oz_rs, ox_ss, ox_rs,
    tz_ss, tz_rs, tx_ss, tx_rs, gz_ss, gz_rs, tg_ss, tg_rs, sw_ss, sw_rs,
):
    a = lax.axis_index("dp")
    t = lax.axis_index("tensor")
    x, z, lo = a // (NZ * NLO), lax.rem(a // NLO, NZ), lax.rem(a, NLO)
    h, c = t // 2, lax.rem(t, 2)
    y = h * NLO + lo
    p = lax.rem(lo, 2)
    q = p * 2 + c
    kk = lo // 2
    n_dp = NX * NZ * NLO
    mine = p == h

    core = ident(x, z, y, 1 - c)
    pair = ident(x, z, y + 1 - 2 * p, c)
    far = ident(x, z, lax.rem(y + NLO, NY), c)
    x_up = ident(lax.rem(x + 1, NX), z, y, c)
    x_dn = ident(lax.rem(x + NX - 1, NX), z, y, c)
    z_up = ident(x, lax.rem(z + 1, NZ), y, c)
    z_dn = ident(x, lax.rem(z + NZ - 1, NZ), y, c)

    last = (lax.rem(a - NLO + n_dp, n_dp), t)
    after = (lax.rem(a + NLO, n_dp), t)

    def ring_y(k):
        return ident(x, z, k, c)

    def when(*conditions):
        live = [k for k in conditions if not isinstance(k, bool)]
        if not all(k for k in conditions if isinstance(k, bool)):
            return lambda body: None
        if not live:
            return lambda body: body()
        both = live[0]
        for k in live[1:]:
            both = both & k
        return pl.when(both)

    takers = [h + 2 * i for i in range(4)]
    holders = [4 * p + l for l in range(NLO)]

    def other(k):
        return jnp.logical_not(k == y)

    def remote(src, dst, ss, rs, device):
        return pltpu.make_async_remote_copy(
            src_ref=src, dst_ref=dst, send_sem=ss, recv_sem=rs, device_id=device, device_id_type=MESH
        )

    def slab(k, rows):
        return pl.ds(k * rows if isinstance(k, int) else pl.multiple_of(k * rows, rows), rows)

    from_next[...] = jnp.zeros((256, D), BF)
    from_last[...] = jnp.zeros((256, D), BF)
    gain = gain_in[...].reshape(1, D)
    h_own[...] = jnp.zeros((16, FW), BF)
    h_own[pl.ds(0, OWN), pl.ds(0, h_in.shape[1])] = h_in[...]
    o_own[...] = jnp.zeros((16, FW), BF)
    turn = lax.broadcasted_iota(jnp.int32, (16, OWN), 0) == lax.broadcasted_iota(jnp.int32, (16, OWN), 1)
    o_own[:, pl.ds(0, o_in.shape[0])] = contract_last(jnp.where(turn, 1.0, 0.0).astype(BF), o_in[...]).astype(BF)

    bar = pltpu.get_barrier_semaphore()

    def signal(device):
        pl.semaphore_signal(bar, inc=1, device_id=device, device_id_type=MESH)

    for device in (core, pair, far, x_up, x_dn, z_up, z_dn, last, after):
        signal(device)
    for k in takers + holders:

        @pl.when(other(k))
        def _():
            signal(ring_y(k))

    pl.semaphore_wait(bar, 17 - 2 * mine.astype(jnp.int32))

    def y_copy(which, src, dst, i):
        to = ident(x, z, h + 2 * i, c)
        return remote(src, dst.at[slab(lo, 16)], y_ss.at[which, i], y_rs.at[which, lo], to)

    def y_sent(which, src, dst):
        for i in range(4):

            @pl.when(jnp.logical_not((h + 2 * i) == y))
            def _():
                y_copy(which, src, dst, i).wait_send()

    def y_wait(which, src, dst):
        for l in range(NLO):

            @pl.when(jnp.logical_not((4 * p + l) == y))
            def _():
                remote(src, dst.at[slab(l, 16)], y_ss.at[which, 0], y_rs.at[which, l], pair).wait_recv()

    for which, (src, dst) in enumerate(((h_own, hy), (o_own, oy))):
        for i in range(4):

            @pl.when(jnp.logical_not((h + 2 * i) == y))
            def _():
                y_copy(which, src, dst, i).start()

            @pl.when((h + 2 * i) == y)
            def _():
                dst[slab(lo, 16), :] = src[...]

        net.sends.append(lambda which=which, src=src, dst=dst: y_sent(which, src, dst))
        net.arrivals["y", which] = lambda which=which, src=src, dst=dst: y_wait(which, src, dst)

    def im_copy(k, block):
        return remote(
            images.at[slab(2 * h + k, 64)], xin.at[slab(2 * k + block, 64)], im_ss.at[k], im_rs.at[k], pair
        )

    for k in range(2):
        net.start(im_copy(k, p), ("im", k), im_copy(k, 1 - p))
        xin[slab(2 * k + p, 64), :] = images[slab(2 * h + k, 64), :]

    tx = text[...].astype(F32)
    text_norm = jnp.sqrt(jnp.sum(tx * tx, axis=1, keepdims=True) + EPS)
    tz[pl.ds(64, 64), :] = (tx / text_norm).astype(BF)
    for d, (device, back) in enumerate(((after, last), (last, after))):
        mine_tz, there, here = tz.at[pl.ds(64, 64)], tz.at[pl.ds(128 * d, 64)], tz.at[pl.ds(128 * d, 64)]
        net.start(
            remote(mine_tz, there, tz_ss.at[d], tz_rs.at[d], device), ("tz", d),
            remote(mine_tz, here, tz_ss.at[d], tz_rs.at[d], back),
        )

    def text_slot(i, d):
        k = i % 2
        used = {(0, 2): lo == 0, (1, 0): lo >= 2, (1, 2): lo <= 2}.get((k, d), True)
        return 4 * d + lo - 2 * k, used

    def tx_copy(i, d):
        j, _ = text_slot(i, d)
        return remote(
            tz.at[pl.ds(64 * d, 64)], texts.at[slab(j, 64)], tx_ss.at[i, d], tx_rs.at[j], ring_y(takers[i])
        )

    def tx_send(d):
        for i in range(4):
            j, used = text_slot(i, d)

            @when(used, other(takers[i]))
            def _():
                tx_copy(i, d).start()

            @when(used, takers[i] == y)
            def _():
                texts[slab(j, 64), :] = tz[pl.ds(64 * d, 64), :]

    def tx_sent():
        for d in range(3):
            for i in range(4):

                @when(text_slot(i, d)[1], other(takers[i]))
                def _():
                    tx_copy(i, d).wait_send()

    def tx_wait():
        for j in range(9):

            @when(jnp.logical_not(mine & (p == j % 4)))
            def _():
                remote(
                    tz.at[pl.ds(64, 64)], texts.at[slab(j, 64)], tx_ss.at[0, 0], tx_rs.at[j], pair
                ).wait_recv()

    tx_send(1)
    net.sends.append(tx_sent)
    net.arrivals["tx"] = tx_wait
    texts[slab(9, 64), :] = jnp.zeros((64, D), BF)

    ring_hx = Ring(net, hx, NX, x, x_up, x_dn, CH48, 1, hx_ss, hx_rs)
    ring_hz = Ring(net, hz, NZ, z, z_up, z_dn, CH144, 2, hz_ss, hz_rs)
    ring_oz = Ring(net, oz, NZ, z, z_up, z_dn, CH48, 1, oz_ss, oz_rs)
    ring_ox = Ring(net, ox, NX, x, x_up, x_dn, CH288, 2, ox_ss, ox_rs)

    pack_y = pack_matrix(NLO, 16, 48, OWN)

    net.wait(("y", 0))
    hx[ring_hx.own(), :] = jnp.dot(pack_y, hy[...], preferred_element_type=F32).astype(BF)
    ring_hx.start()
    for d in (0, 1):
        net.wait(("tz", d))
        tx_send(2 * d)
    net.wait(("y", 1))
    oz[ring_oz.own(), :] = jnp.dot(pack_y, oy[...], preferred_element_type=F32).astype(BF)
    ring_oz.start()
    ring_hx.forward(1)
    ring_oz.forward(1)
    ring_hx.forward(2)
    pack_x = pack_matrix(NX, 48, 144, 4 * OWN)
    hz[ring_hz.own(), :] = jnp.dot(pack_x, hx[...], preferred_element_type=F32).astype(BF)
    ring_oz.forward(2)
    ring_hz.start()
    ring_oz.forward(3)

    @pl.loop(0, 9)
    def _(k):
        rows = lax.broadcasted_iota(jnp.int32, (128, D), 0) + k * 128
        perm[slab(k, 128), :] = jnp.where(rows == order[...], 1.0, 0.0).astype(BF)

    for k in range(2):
        net.wait(("im", k))

    @pl.loop(0, 4)
    def _(r):
        xhat, _ = ln_stats(xin[slab(r, 64), :].astype(F32))
        unit[slab(r, 64), :] = (xhat * gain).astype(BF)

    def permute_normed(cols):
        npm[:, cols] = jnp.dot(unit[...], perm[:, cols], preferred_element_type=F32).astype(BF)

    column_loop(permute_normed)

    ring_oz.forward(4)

    def pack_ox(cols):
        pack_z = pack_matrix(NZ, 48, 288, 4 * OWN)
        ox[ring_ox.own(), cols] = jnp.dot(pack_z, oz[:, cols], preferred_element_type=F32).astype(BF)

    column_loop(pack_ox)
    ring_ox.start()
    ring_hz.forward(1)
    ring_hz.forward(2)
    ring_ox.forward(1)
    ring_hz.forward(3)
    ring_hz.forward(4)

    def hidden(cols):
        v = jnp.dot(npm[...], hz[:, cols], preferred_element_type=F32)
        preact[:, cols] = v
        act[:, cols] = (0.5 * v * (1.0 + jnp.tanh(GELU_C * (v + GELU_A * (v * v * v))))).astype(BF)

    column_loop(hidden)
    ring_ox.forward(2)

    def head_terms(cols):
        part[:, cols] = contract_last(act[...], ox[cols, :])

    column_loop(head_terms)

    own_rows = slab(c, 128)
    other_rows = slab(1 - c, 128)

    def swap(n, src, dst, device, comes=None):
        def copy(src, dst):
            return remote(src, dst, sw_ss.at[n], sw_rs.at[n], device)

        net.start(copy(src, dst), n, comes is not None and copy(comes, comes))

    def core_sum(n, k):
        cs[slab(k, 128), :] = part[other_rows, :].astype(BF)
        swap(n, cs.at[slab(k, 128)], cr.at[slab(k, 128)], core)
        net.wait(n)
        accb[...] = part[own_rows, :] + cr[slab(k, 128), :].astype(F32)

    core_sum(0, 0)
    es[slab(0, 128), :] = accb[...].astype(BF)
    swap(1, es.at[slab(0, 128)], er.at[slab(0, 128)], pair)

    def gelu_slope(cols):
        v = preact[:, cols]
        th = jnp.tanh(GELU_C * (v + GELU_A * (v * v * v)))
        inner = GELU_C * (1.0 + (3.0 * GELU_A) * (v * v))
        dgel[:, cols] = 0.5 * (1.0 + th) + 0.5 * v * (1.0 - th * th) * inner

    column_loop(gelu_slope)
    net.wait(1)

    @pl.loop(0, 2)
    def _(b):
        rows = slab(b, 64)
        out = xin[slab(2 * c + b, 64), :].astype(F32) + accb[rows, :] + er[rows, :].astype(F32)
        norm = jnp.sqrt(jnp.sum(out * out, axis=1, keepdims=True) + EPS)
        out = out / norm
        head[rows, :] = out
        inorm[rows, :] = jnp.broadcast_to(norm, (64, 128))
        unit[slab(2 * c + b, 64), :] = out.astype(BF)

    swap(2, unit.at[own_rows], unit.at[own_rows], core, unit.at[other_rows])
    net.wait("tx")
    net.wait(2)

    own_quarter = 2 * h

    def slope(dots, row, col):
        block = lax.shift_right_logical(row, 6) & 1
        scored = (col >= block * 64) & (col < 512 + block * 64)
        match = (col == 256 + block * 64 + (row & 63)) & (lax.shift_right_logical(row, 7) + own_quarter == q)
        value = jax.nn.sigmoid(SCALE_LOGIT * dots + BIAS_LOGIT) - jnp.where(match, 1.0, 0.0)
        return jnp.where(scored, SCALE_LOGIT * value, 0.0).astype(BF)

    @pl.loop(0, 5)
    def _(k):
        cols = slab(k, 128)
        row = lax.broadcasted_iota(jnp.int32, (256, 128), 0)
        col = lax.broadcasted_iota(jnp.int32, (256, 128), 1) + k * 128
        slopes[:, cols] = slope(contract_last(unit[...], texts[cols, :]), row, col)

    def to_image(cols):
        part[:, cols] = jnp.dot(slopes[...], texts[:, cols], preferred_element_type=F32)

    column_loop(to_image)
    core_sum(3, 1)
    es[slab(1, 128), :] = accb[...].astype(BF)
    swap(4, es.at[slab(1, 128)], er.at[slab(1, 128)], pair)

    @pl.loop(0, 5)
    def _(k):
        rows = slab(k, 128)
        row = lax.broadcasted_iota(jnp.int32, (128, 256), 1)
        col = lax.broadcasted_iota(jnp.int32, (128, 256), 0) + k * 128
        slopes_t[rows, :] = slope(contract_last(texts[rows, :], unit[...]), row, col)

    def to_text(cols):
        tgs[:, cols] = jnp.dot(slopes_t[...], unit[:, cols], preferred_element_type=F32).astype(BF)

    column_loop(to_text)
    net.wait(4)

    @pl.loop(0, 2)
    def _(b):
        rows = slab(b, 64)
        g = accb[rows, :] + er[pl.ds(pl.multiple_of(128 + b * 64, 64), 64), :].astype(F32)
        f = head[rows, :]
        out = (g - f * jnp.sum(f * g, axis=1, keepdims=True)) / inorm[rows, 0:1]
        gout[rows, :] = out
        gob[slab(2 * c + b, 64), :] = out.astype(BF)

    swap(5, gob.at[own_rows], gob.at[own_rows], core, gob.at[other_rows])

    def gz_each(pick, act):
        for k in range(2):
            for d, device, buf in ((0, last, from_next), (1, after, from_last)):
                for r in range(NLO):
                    j = 8 * d + r - 2 * k
                    if 0 <= j <= 8 and pick(r):

                        @pl.when(kk == k)
                        def _():
                            there = buf.at[pl.ds(64 * r, 64)]
                            act(remote(tgs.at[pl.ds(64 * j, 64)], there, gz_ss.at[d, r], gz_rs.at[d, r], device))

    gz_each(lambda r: True, lambda copy: copy.start())
    net.sends.append(lambda: gz_each(lambda r: True, lambda copy: copy.wait_send()))
    for r in range(NLO):
        net.arrivals["gz", r] = lambda r=r: gz_each(lambda k: k == r, lambda copy: copy.wait_recv())

    def tg_copy(r):
        return remote(
            tgy.at[pl.ds(64 * r, 64)], tgr.at[slab(y // 2, 64)], tg_ss.at[r], tg_rs.at[y // 2], ring_y(holders[r])
        )

    def tg_send(r):
        net.wait(("gz", r))
        rows = pl.ds(64 * r, 64)
        own = tgs[slab(4 + r - 2 * kk, 64), :].astype(F32)
        total = (own + from_next[rows, :].astype(F32) + from_last[rows, :].astype(F32)).astype(BF)
        tgy[rows, :] = total

        @pl.when(other(holders[r]))
        def _():
            tg_copy(r).start()

        @pl.when(holders[r] == y)
        def _():
            tgr[slab(y // 2, 64), :] = total

    def tg_sent():
        for r in range(NLO):

            @pl.when(other(holders[r]))
            def _():
                tg_copy(r).wait_send()

    def tg_wait():
        for i in range(4):

            @pl.when(other(takers[i]))
            def _():
                remote(
                    tgy.at[pl.ds(0, 64)], tgr.at[pl.ds(64 * i, 64)], tg_ss.at[0], tg_rs.at[i], pair
                ).wait_recv()

    net.wait(5)

    def hidden_back(cols):
        g = jnp.dot(gob[...], ox[:, cols], preferred_element_type=F32)
        gpre[:, cols] = (g * dgel[:, cols]).astype(BF)

    column_loop(hidden_back)
    for r in range(NLO):
        tg_send(r)
    net.sends.append(tg_sent)
    net.arrivals["tg"] = tg_wait

    def normed_terms(cols):
        part[:, cols] = contract_last(gpre[...], hz[cols, :])

    column_loop(normed_terms)
    core_sum(6, 2)
    es[pl.ds(256, 64), :] = accb[slab(1 - p, 64), :].astype(BF)
    swap(7, es.at[pl.ds(256, 64)], er.at[pl.ds(256, 64)], pair)
    xhat, rdev = ln_stats(xin[slab(2 * c + p, 64), :].astype(F32))
    net.wait(7)
    total = accb[slab(p, 64), :] + er[pl.ds(256, 64), :].astype(F32)
    high = total.astype(BF)
    low = (total - high.astype(F32)).astype(BF)

    @pl.loop(0, 3)
    def _(k):
        cols = pl.ds(pl.multiple_of(k * 384, 128), 384)
        gnat[:, cols] = contract_last(high, perm[cols, :]) + contract_last(low, perm[cols, :])

    g = gnat[...] * gain
    mean_g = jnp.sum(g, axis=1, keepdims=True) * (1.0 / D)
    mean_gx = jnp.sum(g * xhat, axis=1, keepdims=True) * (1.0 / D)
    done = slab(2 * h + c, 64)
    out_img[done, :] = (gout[slab(p, 64), :] + rdev * (g - mean_g - xhat * mean_gx)).astype(BF)
    from_far, from_core, from_both = slab(2 * (1 - h) + c, 64), slab(2 * h + 1 - c, 64), slab(2 * (1 - h) + 1 - c, 64)
    swap(8, out_img.at[done], out_img.at[done], far, out_img.at[from_far])
    swap(9, out_img.at[done], out_img.at[done], core, out_img.at[from_core])

    net.wait("tg")
    g = tgr[pl.ds(0, 64), :].astype(F32)
    for k in range(1, 4):
        g = g + tgr[slab(k, 64), :].astype(F32)
    tx = text[...].astype(F32)
    text_norm = jnp.sqrt(jnp.sum(tx * tx, axis=1, keepdims=True) + EPS)
    text_f = tx / text_norm
    out_text[...] = (g - text_f * jnp.sum(text_f * g, axis=1, keepdims=True)) / text_norm
    net.wait(8)
    swap(10, out_img.at[from_far], out_img.at[from_far], core, out_img.at[from_both])


def kernel(*refs):
    net = Net()
    stages(net, *refs)
    net.drain()


def feature_order():
    z, x, j = np.meshgrid(np.arange(NZ), np.arange(NX), np.arange(NLO * OWN), indexing="ij")
    return (x * (NZ * NLO * OWN) + z * (NLO * OWN) + j).reshape(1, D).astype(np.int32)


def shards(images, layer_norm_gain, hidden_weight, output_weight, text):

    def vm(rows, cols, kind=BF):
        return pltpu.VMEM((rows, cols), kind)

    dma = pltpu.SemaphoreType.DMA
    scratch = [
        vm(16, FW), vm(16, FW), vm(64, FW), vm(64, FW), vm(192, FW), vm(D, FW), vm(384, FW), vm(D, FW),
        vm(256, D), vm(D, D), vm(256, D), vm(256, FW), vm(256, FW, F32), vm(256, FW, F32), vm(256, D, F32),
        vm(384, D), vm(384, D), vm(320, D), vm(320, D),
        vm(256, D), vm(128, D, F32), vm(128, 128, F32), vm(128, D, F32), vm(256, D), vm(256, FW),
        vm(640, D), vm(192, D), vm(640, D), vm(256, D), vm(256, D), vm(256, D), vm(256, D), vm(256, 640), vm(640, 256), vm(128, D, F32), vm(64, D, F32),
        dma((2, 4)), dma((2, 4)), dma((2,)), dma((2,)),
        dma((2, 2, 2)), dma((2, 2, 2)), dma((4, 2, 4)), dma((4, 2, 4)),
        dma((4, 2, 2)), dma((4, 2, 2)), dma((2, 2, 4)), dma((2, 2, 4)),
        dma((2,)), dma((2,)), dma((4, 3)), dma((9,)), dma((2, 4)), dma((2, 4)), dma((4,)), dma((4,)), dma((11,)), dma((11,)),
    ]
    vmem = pl.BlockSpec(memory_space=pltpu.VMEM)
    images_gradient, grad_text = pl.pallas_call(
        kernel,
        out_shape=(jax.ShapeDtypeStruct((256, D), BF), jax.ShapeDtypeStruct((64, D), F32)),
        in_specs=[vmem] * 6,
        out_specs=(vmem, vmem),
        scratch_shapes=scratch,
        compiler_params=pltpu.CompilerParams(
            collective_id=0, has_side_effects=True, vmem_limit_bytes=56 * 2**20
        ),
        cost_estimate=pl.CostEstimate(flops=4 * 10**9, bytes_accessed=4 * 10**6, transcendentals=10**6),
    )(images, layer_norm_gain, hidden_weight, output_weight, text, jnp.asarray(feature_order()))
    return images_gradient.astype(F32), grad_text


def solution(mesh):
    placed = (P("dp", None), P(), P("dp", "tensor"), P("tensor", "dp"), P(("dp", "tensor"), None))
    return jax.shard_map(
        shards,
        mesh=mesh,
        in_specs=placed,
        out_specs=(P("dp", None), P(("dp", "tensor"), None)),
        check_vma=False,
    )
```

time: 174 us -> 147 us (0.84)
  Pallas kernels: 166 us -> 142 us
  local copies, waits for them, and re-layouts: 4.79 us -> 2.37 us
    pallas_call x1, Pallas kernels: 166 us -> 142 us  [shards(): pl.pallas_call(kernel, out_shape=(jax.ShapeDtypeStruct((256, D), BF), jax...]
    pad x2 -> x0, local copies, waits for them, and re-layouts: 2.78 us -> none  [the longest x1 1.39 us: shards(): h_own = jnp.pad(hidden_weight, pad)]
where the time goes in v2:
time: 147 us
  Pallas kernels  142 us (97%)
  local copies, waits for them, and re-layouts  2.37 us (2%)
  other arithmetic  2.2 us (1%)
    pallas_call x1, Pallas kernels, shards(): pl.pallas_call(kernel, out_shape=(jax.ShapeDtypeStruct((256, D), BF), jax...  142 us

profile of v2, /device:TPU:25, one launch (start us, length us, event | category | flops | bytes accessed | tf_op | source)
XLA Modules:
  0.0 147.0 jit_solution(16795473141908904470)
XLA Ops:
  0.6 1.7 %copy.8.refs_3_ = bf16[1076,9]{1,0:T(8,128)(2,1)} copy(bf16[1076,9]{0,1:T(8,128)(2,1)} %param.9) | data formatting | bytes 38736 | tf_op args[3]
  2.3 141.8 %shard_map.77 = (bf16[256,1152]{1,0:T(8,128)(2,1)}, f32[64,1152]{1,0:T(8,128)}) custom-call(bf16[256,1152]{1,0:T(8,128)(2,1)} %refs_0_.1, f32[1152]{0:T(1024)} %refs_1_.1, bf16[9,1076]{1,0:T(8,128)(2,1)} %refs_2_.1, bf16[1076,9]{1,0:T(8,128)(2,1)} %copy.8.refs_3_, bf16[64,1152]{1,0:T(8,128)(2,1)} %refs_4_.1, s32[1,1152]{1,0:T(1,128)} %constant.2.clone.refs_5_), custom_call_target="tpu_custom_call" | custom-call | flops 4000000000 | bytes 4000000 | tf_op jit(solution)/shard_map/pallas_call | solution.py:604
  144.1 0.0 copy-start
  144.1 2.2 %convert_element_type.3 = f32[256,1152]{1,0:T(8,128)} convert(bf16[256,1152]{1,0:T(8,128)(2,1)} %get-tuple-element.4) | non-fusion elementwise | flops 294912 | bytes 1769472 | tf_op jit(solution)/shard_map/convert_element_type | solution.py:615
  146.3 0.0 copy-done
  146.3 0.7 copy.10
Async XLA Ops:
  144.1 2.2 %copy-start = (f32[64,1152]{1,0:T(8,128)S(1)}, f32[64,1152]{1,0:T(8,128)}, u32[]{:S(2)}) copy-start(f32[64,1152]{1,0:T(8,128)} %get-tuple-element.9) | copy-start | bytes 884740

commit v3 on v2

v3 whole, which is shorter than its diff:
```python
import jax
import jax.numpy as jnp
import numpy as np
from jax import lax
from jax.experimental import pallas as pl
from jax.experimental.pallas import tpu as pltpu
from jax.sharding import PartitionSpec as P

SCALE_LOGIT = 10.0
BIAS_LOGIT = -3.0
EPS = 1e-06

NX, NZ, NY, NLO = 4, 8, 8, 4
D = 1152
FW = 1152
MAIN, REST = 32, 4
FOLDS = ((0, 640), (640, 512), (1152, 640), (1792, 512))
OWN = 9
ARRIVALS = (
    ("Az", 0, 1), ("Bx", 0, 1), ("Bz", 0, 1), ("Ax", 0, 1), ("Bx", 0, 2), ("Az", 0, 2), ("Bx", -1, 1), ("Bz", 0, 2),
    ("Az", -1, 1), ("Bx", 1, 1), ("Ax", 0, 2), ("Az", 1, 1), ("Bx", -1, 2), ("Az", 0, 3), ("Bx", -2, 1), ("Bz", 0, 3),
    ("Bx", 2, 1), ("Az", -1, 2), ("Bx", 1, 2), ("Bx", -2, 2), ("Az", 2, 1), ("Az", 1, 2), ("Bx", -3, 1), ("Az", 0, 4),
    ("Bz", 0, 4), ("Bx", 3, 1), ("Bx", 2, 2), ("Az", -1, 3), ("Bx", -3, 2), ("Az", 2, 2), ("Bx", 4, 1), ("Az", 1, 3),
    ("Bx", 3, 2), ("Az", -1, 4), ("Bx", 4, 2), ("Az", 2, 3), ("Az", 1, 4), ("Az", 2, 4),
)
MESH = pl.DeviceIdType.MESH
BF = jnp.bfloat16
F32 = jnp.float32
GELU_C = 0.7978845608028654
GELU_A = 0.044715


def contract_last(left, right):
    return lax.dot_general(left, right, (((1,), (1,)), ((), ())), preferred_element_type=F32)


def ident(x, z, y, c):
    return (x * (NZ * NLO) + z * NLO + lax.rem(y, NLO), (y // NLO) * 2 + c)


class Net:
    def __init__(self):
        self.sends, self.arrivals = [], {}

    def start(self, copy, name, arrival=None):
        copy.start()
        self.sends.append(copy.wait_send)
        self.arrivals[name] = (arrival or copy).wait_recv

    def wait(self, name):
        self.arrivals.pop(name)()

    def drain(self):
        for name in list(self.arrivals):
            self.wait(name)
        for wait_send in self.sends:
            wait_send()


class Ring:
    def __init__(self, net, buf, rows, size, pos, at, peers, sems, last):
        self.net, self.buf, self.rows, self.size, self.pos, self.at = net, buf, rows, size, pos, at
        self.peers, self.sems, self.last = peers, sems, last
        self.steps = size // 2

    def part(self, step, way):
        if step < self.steps:
            return 0, self.rows
        if self.last is None:
            return way * (self.rows // 2), self.rows // 2
        return (0, self.rows) if way == self.last else None

    def copy(self, step, way, back):
        slot = lax.rem(self.pos + (-back if way == 0 else back) + 2 * self.size, self.size)
        off, rows = self.part(step, way)
        ref = self.buf.at[pl.ds(pl.multiple_of(self.at(slot) + off, 16), rows)]
        ssem, rsem = self.sems(step - 1, way)
        return pltpu.make_async_remote_copy(
            src_ref=ref, dst_ref=ref, send_sem=ssem, recv_sem=rsem, device_id=self.peers[way], device_id_type=MESH
        )

    def send(self, step):
        for way in (0, 1):
            if self.part(step, way):
                self.go(step, way)

    def go(self, step, way):
        self.net.start(self.copy(step, way, step - 1), (self, step, way), self.copy(step, way, step))

    def forward(self, step):
        for way in (0, 1):
            if self.part(step, way):
                self.net.wait((self, step, way))
                if step < self.steps and self.part(step + 1, way):
                    self.go(step + 1, way)


def pick_matrix(rows, cols, pairs):
    row = lax.broadcasted_iota(jnp.int32, (rows, cols), 0)
    col = lax.broadcasted_iota(jnp.int32, (rows, cols), 1)
    hit = jnp.zeros((rows, cols), F32)
    for test in pairs:
        hit = jnp.where(test(row, col), 1.0, hit)
    return hit.astype(BF)


def column_loop(body):
    @pl.loop(0, 3)
    def _(k):
        body(pl.ds(pl.multiple_of(k * 384, 128), 384))


def ln_stats(v):
    v = v - jnp.sum(v, axis=1, keepdims=True) * (1.0 / D)
    var = jnp.sum(v * v, axis=1, keepdims=True) * (1.0 / D)
    rdev = 1.0 / jnp.sqrt(var + EPS)
    return v * rdev, rdev


def stages(
    net, images, gain_in, h_in, o_in, text, order,
    out_img, out_text,
    w_own, wy, hm, om, rest, xin, xp, perm, npm, gperm, act, preact, dgel, part,
    cs, cr, es, er, unit, head, inorm, gout, gob, gpre, texts, tz, tgs, from_next, from_last, tgy, tgr, slopes, slopes_t, accb, tp,
    y_ss, y_rs, im_ss, im_rs, ax_ss, ax_rs, az_ss, az_rs, bz_ss, bz_rs, bx_ss, bx_rs,
    tz_ss, tz_rs, tx_ss, tx_rs, gz_ss, gz_rs, tg_ss, tg_rs, sw_ss, sw_rs,
):
    a = lax.axis_index("dp")
    t = lax.axis_index("tensor")
    x, z, lo = a // (NZ * NLO), lax.rem(a // NLO, NZ), lax.rem(a, NLO)
    h, c = t // 2, lax.rem(t, 2)
    y = h * NLO + lo
    p = lax.rem(lo, 2)
    q = p * 2 + c
    kk = lo // 2
    n_dp = NX * NZ * NLO
    mine = p == h

    core = ident(x, z, y, 1 - c)
    pair = ident(x, z, y + 1 - 2 * p, c)
    far = ident(x, z, lax.rem(y + NLO, NY), c)
    x_up = ident(lax.rem(x + 1, NX), z, y, c)
    x_dn = ident(lax.rem(x + NX - 1, NX), z, y, c)
    z_up = ident(x, lax.rem(z + 1, NZ), y, c)
    z_dn = ident(x, lax.rem(z + NZ - 1, NZ), y, c)

    last = (lax.rem(a - NLO + n_dp, n_dp), t)
    after = (lax.rem(a + NLO, n_dp), t)

    def ring_y(k):
        return ident(x, z, k, c)

    def when(*conditions):
        live = [k for k in conditions if not isinstance(k, bool)]
        if not all(k for k in conditions if isinstance(k, bool)):
            return lambda body: None
        if not live:
            return lambda body: body()
        both = live[0]
        for k in live[1:]:
            both = both & k
        return pl.when(both)

    takers = [h + 2 * i for i in range(4)]
    holders = [4 * p + l for l in range(NLO)]

    def other(k):
        return jnp.logical_not(k == y)

    def remote(src, dst, ss, rs, device):
        return pltpu.make_async_remote_copy(
            src_ref=src, dst_ref=dst, send_sem=ss, recv_sem=rs, device_id=device, device_id_type=MESH
        )

    def slab(k, rows):
        return pl.ds(k * rows if isinstance(k, int) else pl.multiple_of(k * rows, rows), rows)

    from_next[...] = jnp.zeros((256, D), BF)
    from_last[...] = jnp.zeros((256, D), BF)
    width = h_in.shape[1]
    turn = pick_matrix(16, OWN, [lambda row, col: row == col])
    w_own[...] = jnp.zeros((16, 2 * FW), BF)
    w_own[pl.ds(0, OWN), pl.ds(0, width)] = h_in[...]
    w_own[:, pl.ds(FW, width)] = contract_last(turn, o_in[...]).astype(BF)

    bar = pltpu.get_barrier_semaphore()

    def signal(device):
        pl.semaphore_signal(bar, inc=1, device_id=device, device_id_type=MESH)

    for device in (core, pair, far, x_up, x_dn, z_up, z_dn, last, after):
        signal(device)
    for k in takers + holders:

        @pl.when(other(k))
        def _():
            signal(ring_y(k))

    pl.semaphore_wait(bar, 17 - 2 * mine.astype(jnp.int32))

    def y_copy(i):
        return remote(w_own, wy.at[slab(lo, 16)], y_ss.at[i], y_rs.at[lo], ring_y(takers[i]))

    def y_sent():
        for i in range(4):

            @pl.when(other(takers[i]))
            def _():
                y_copy(i).wait_send()

    def y_wait():
        for l in range(NLO):

            @pl.when(other(holders[l]))
            def _():
                remote(w_own, wy.at[slab(l, 16)], y_ss.at[0], y_rs.at[l], pair).wait_recv()

    for i in range(4):

        @pl.when(other(takers[i]))
        def _():
            y_copy(i).start()

        @pl.when(takers[i] == y)
        def _():
            wy[slab(lo, 16), :] = w_own[...]

    net.sends.append(y_sent)
    net.arrivals["y"] = y_wait

    @pl.loop(0, 9)
    def _(k):
        rows = lax.broadcasted_iota(jnp.int32, (128, D), 0) + k * 128
        perm[slab(k, 128), :] = jnp.where(rows == order[...], 1.0, 0.0).astype(BF)

    gain = gain_in[...].reshape(1, D)
    high = gain.astype(BF)
    middle = (gain - high.astype(F32)).astype(BF)
    low = (gain - high.astype(F32) - middle.astype(F32)).astype(BF)
    three = jnp.concatenate([high, middle, low, jnp.zeros((13, D), BF)], axis=0)

    def permute_text(cols):
        terms = jnp.dot(three, perm[:, cols], preferred_element_type=F32)
        gperm[:, cols] = jnp.sum(terms, axis=0, keepdims=True)
        tp[:, cols] = jnp.dot(text[...], perm[:, cols], preferred_element_type=F32).astype(BF)

    column_loop(permute_text)

    tx = tp[...].astype(F32)
    text_norm = jnp.sqrt(jnp.sum(tx * tx, axis=1, keepdims=True) + EPS)
    tz[pl.ds(64, 64), :] = (tx / text_norm).astype(BF)
    for d, (device, back) in enumerate(((after, last), (last, after))):
        mine_tz, there, here = tz.at[pl.ds(64, 64)], tz.at[pl.ds(128 * d, 64)], tz.at[pl.ds(128 * d, 64)]
        net.start(
            remote(mine_tz, there, tz_ss.at[d], tz_rs.at[d], device), ("tz", d),
            remote(mine_tz, here, tz_ss.at[d], tz_rs.at[d], back),
        )

    def text_slot(i, d):
        k = i % 2
        used = {(0, 2): lo == 0, (1, 0): lo >= 2, (1, 2): lo <= 2}.get((k, d), True)
        return 4 * d + lo - 2 * k, used

    def tx_copy(i, d):
        j, _ = text_slot(i, d)
        return remote(
            tz.at[pl.ds(64 * d, 64)], texts.at[slab(j, 64)], tx_ss.at[i, d], tx_rs.at[j], ring_y(takers[i])
        )

    def tx_send(i, d):
        j, used = text_slot(i, d)

        @when(used, other(takers[i]))
        def _():
            tx_copy(i, d).start()

        @when(used, takers[i] == y)
        def _():
            texts[slab(j, 64), :] = tz[pl.ds(64 * d, 64), :]

    def tx_sent():
        for d in range(3):
            for i in range(4):

                @when(text_slot(i, d)[1], other(takers[i]))
                def _():
                    tx_copy(i, d).wait_send()

    def tx_wait():
        for j in range(9):

            @when(jnp.logical_not(mine & (p == j % 4)))
            def _():
                remote(
                    tz.at[pl.ds(64, 64)], texts.at[slab(j, 64)], tx_ss.at[0, 0], tx_rs.at[j], pair
                ).wait_recv()

    net.sends.append(tx_sent)
    net.arrivals["tx"] = tx_wait
    texts[slab(9, 64), :] = jnp.zeros((64, D), BF)

    def place(x_at, z_at, rows):
        return (x_at * NZ + z_at) * rows

    def x_of(rel):
        return lax.rem(x + rel + NX, NX)

    def z_of(rel):
        return lax.rem(z + rel + NZ, NZ)

    rings = {}

    def ring(key, buf, rows, size, pos, at, peers, ss, rs, last):
        rings.setdefault(key, []).append(
            Ring(net, buf, rows, size, pos, at, peers, lambda step, way: (ss.at[step, way], rs.at[step, way]), last)
        )

    ups, zs = (x_up, x_dn), (z_up, z_dn)
    ring(("Ax", 0), hm, MAIN, NX, x, lambda k: place(k, z, MAIN), ups, ax_ss, ax_rs, None)
    for n, rel in enumerate((0, -1, 1, 2)):
        ring(
            ("Az", rel), hm, MAIN, NZ, z, lambda k, rel=rel: place(x_of(rel), k, MAIN), zs,
            az_ss.at[n], az_rs.at[n], None,
        )
    for n, (buf, rows) in enumerate(((om, MAIN), (rest, 16))):
        ring(
            ("Bz", 0), buf, rows, NZ, z, lambda k, rows=rows: place(x, k, rows), zs,
            bz_ss.at[n], bz_rs.at[n], 0 if n else None,
        )
        for m, rel in enumerate((0, -1, 1, -2, 2, -3, 3, 4)):
            ring(
                ("Bx", rel), buf, rows, NX, x, lambda k, rel=rel, rows=rows: place(k, z_of(rel), rows), ups,
                bx_ss.at[n, m], bx_rs.at[n, m], m % 2 if n else None,
            )

    def begin(key):
        for one in rings[key]:
            one.send(1)

    net.wait("y")
    keep = pick_matrix(MAIN, 64, [lambda row, col: row == lax.shift_right_logical(col, 4) * OWN + (col & 15)])
    keep = jnp.where((lax.broadcasted_iota(jnp.int32, (MAIN, 64), 1) & 15) < OWN, keep, jnp.zeros_like(keep))
    mine_main = pl.ds(pl.multiple_of(place(x, z, MAIN), MAIN), MAIN)
    hm[mine_main, :] = jnp.dot(keep, wy[:, pl.ds(0, FW)], preferred_element_type=F32).astype(BF)
    begin(("Az", 0))
    om[mine_main, :] = jnp.dot(keep, wy[:, pl.ds(FW, FW)], preferred_element_type=F32).astype(BF)
    folded = jnp.zeros((16, 640), F32)
    for u, (lane, lanes) in enumerate(FOLDS):
        pick = pick_matrix(16, 64, [lambda row, col: ((row & 3) == u) & (col == 48 + 5 + lax.shift_right_logical(row, 2))])
        got = jnp.dot(pick, wy[:, pl.ds(lane, lanes)], preferred_element_type=F32)
        if lanes < 640:
            got = jnp.concatenate([got, jnp.zeros((16, 640 - lanes), F32)], axis=1)
        folded = folded + got
    rest[pl.ds(pl.multiple_of(place(x, z, 16), 16), 16), :] = folded.astype(BF)
    for key in (("Bz", 0), ("Bx", 0), ("Ax", 0)):
        begin(key)

    def im_copy(k, block):
        return remote(
            images.at[slab(2 * h + k, 64)], xin.at[slab(2 * k + block, 64)], im_ss.at[k], im_rs.at[k], pair
        )

    for k in range(2):
        net.start(im_copy(k, p), ("im", k), im_copy(k, 1 - p))
        xin[slab(2 * k + p, 64), :] = images[slab(2 * h + k, 64), :]

    sends = [lambda i=i: tx_send(i, 1) for i in range(4)]
    sends += [lambda: net.wait(("tz", 0)), lambda: net.wait(("tz", 1))]
    sends += [lambda i=i, d=d: tx_send(i, d) for d in (0, 2) for i in range(4)]

    def normed_rows():
        for k in range(2):
            net.wait(("im", k))

        def permute_images(cols):
            xp[:, cols] = jnp.dot(xin[...], perm[:, cols], preferred_element_type=F32).astype(BF)

        column_loop(permute_images)

        @pl.loop(0, 4)
        def _(r):
            xhat, _ = ln_stats(xp[slab(r, 64), :].astype(F32))
            npm[slab(r, 64), :] = (xhat * gperm[...]).astype(BF)

    for n, (route, rel, step) in enumerate(ARRIVALS):
        for one in rings[route, rel]:
            one.forward(step)
        if route == "Ax":
            for k in ((-1, 1), (2,))[step - 1]:
                begin(("Az", k))
        if route == "Bz":
            for k in (-step, step) if step < 4 else (4,):
                begin(("Bx", k))
        if n % 2 == 0 and sends:
            sends.pop(0)()
        if n == 30:
            normed_rows()

    def unfold(u, buf, lane, lanes):
        tests = [lambda row, col: col == lax.shift_right_logical(row, 2) * 16 + (row & 3) * 4 + u]
        got = jnp.dot(pick_matrix(128, 512, tests), rest[:, pl.ds(0, lanes)], preferred_element_type=F32)
        buf[pl.ds(1024, 128), pl.ds(lane, lanes)] = got.astype(BF)

    for u, (lane, lanes) in enumerate(FOLDS):
        unfold(u, hm if lane < FW else om, lane % FW, lanes)

    def hidden(cols):
        v = jnp.dot(npm[...], hm[:, cols], preferred_element_type=F32)
        preact[:, cols] = v
        act[:, cols] = (0.5 * v * (1.0 + jnp.tanh(GELU_C * (v + GELU_A * (v * v * v))))).astype(BF)

    column_loop(hidden)

    def head_terms(cols):
        part[:, cols] = contract_last(act[...], om[cols, :])

    column_loop(head_terms)

    def swap(n, src, dst, device, comes=None):
        def copy(src, dst):
            return remote(src, dst, sw_ss.at[n], sw_rs.at[n], device)

        net.start(copy(src, dst), n, comes is not None and copy(comes, comes))

    def core_send(n, k, at, b):
        rows = pl.ds(128 * k + 64 * at, 64)
        cs[rows, :] = part[slab(2 * (1 - c) + b, 64), :].astype(BF)
        swap(n + at, cs.at[rows], cr.at[rows], core)

    def core_add(n, k, at, b):
        net.wait(n + at)
        rows = pl.ds(128 * k + 64 * at, 64)
        accb[slab(b, 64), :] = part[slab(2 * c + b, 64), :] + cr[rows, :].astype(F32)

    def pair_send(n, k, at, b):
        rows = pl.ds(128 * k + 64 * at, 64)
        es[rows, :] = accb[slab(b, 64), :].astype(BF)
        swap(n + at, es.at[rows], er.at[rows], pair)

    def sum_start(n, k):
        for b in range(2):
            core_send(n, k, b, b)
        for b in range(2):
            core_add(n, k, b, b)
            pair_send(n + 2, k, b, b)

    def sum_end(n, k, b):
        net.wait(n + 2 + b)
        return accb[slab(b, 64), :] + er[pl.ds(128 * k + 64 * b, 64), :].astype(F32)

    def share(n, ref, b):
        rows, comes = slab(2 * c + b, 64), slab(2 * (1 - c) + b, 64)
        swap(n + b, ref.at[rows], ref.at[rows], core, ref.at[comes])

    sum_start(0, 0)

    def gelu_slope(cols):
        v = preact[:, cols]
        th = jnp.tanh(GELU_C * (v + GELU_A * (v * v * v)))
        inner = GELU_C * (1.0 + (3.0 * GELU_A) * (v * v))
        dgel[:, cols] = 0.5 * (1.0 + th) + 0.5 * v * (1.0 - th * th) * inner

    column_loop(gelu_slope)
    for b in range(2):
        rows = slab(b, 64)
        out = xp[slab(2 * c + b, 64), :].astype(F32) + sum_end(0, 0, b)
        norm = jnp.sqrt(jnp.sum(out * out, axis=1, keepdims=True) + EPS)
        out = out / norm
        head[rows, :] = out
        inorm[rows, :] = jnp.broadcast_to(norm, (64, 128))
        unit[slab(2 * c + b, 64), :] = out.astype(BF)
        share(4, unit, b)
    net.wait("tx")
    for b in range(2):
        net.wait(4 + b)

    own_quarter = 2 * h

    def slope(dots, row, col):
        block = lax.shift_right_logical(row, 6) & 1
        scored = (col >= block * 64) & (col < 512 + block * 64)
        match = (col == 256 + block * 64 + (row & 63)) & (lax.shift_right_logical(row, 7) + own_quarter == q)
        value = jax.nn.sigmoid(SCALE_LOGIT * dots + BIAS_LOGIT) - jnp.where(match, 1.0, 0.0)
        return jnp.where(scored, SCALE_LOGIT * value, 0.0).astype(BF)

    @pl.loop(0, 5)
    def _(k):
        cols = slab(k, 128)
        row = lax.broadcasted_iota(jnp.int32, (256, 128), 0)
        col = lax.broadcasted_iota(jnp.int32, (256, 128), 1) + k * 128
        slopes[:, cols] = slope(contract_last(unit[...], texts[cols, :]), row, col)

    def to_image(cols):
        part[:, cols] = jnp.dot(slopes[...], texts[:, cols], preferred_element_type=F32)

    column_loop(to_image)
    sum_start(6, 1)

    @pl.loop(0, 5)
    def _(k):
        rows = slab(k, 128)
        row = lax.broadcasted_iota(jnp.int32, (128, 256), 1)
        col = lax.broadcasted_iota(jnp.int32, (128, 256), 0) + k * 128
        slopes_t[rows, :] = slope(contract_last(texts[rows, :], unit[...]), row, col)

    def to_text(cols):
        tgs[:, cols] = jnp.dot(slopes_t[...], unit[:, cols], preferred_element_type=F32).astype(BF)

    column_loop(to_text)
    def gz_each(pick, act):
        for k in range(2):
            for d, device, buf in ((0, last, from_next), (1, after, from_last)):
                for r in range(NLO):
                    j = 8 * d + r - 2 * k
                    if 0 <= j <= 8 and pick(r):

                        @pl.when(kk == k)
                        def _():
                            there = buf.at[pl.ds(64 * r, 64)]
                            act(remote(tgs.at[pl.ds(64 * j, 64)], there, gz_ss.at[d, r], gz_rs.at[d, r], device))

    gz_each(lambda r: True, lambda copy: copy.start())
    net.sends.append(lambda: gz_each(lambda r: True, lambda copy: copy.wait_send()))
    for r in range(NLO):
        net.arrivals["gz", r] = lambda r=r: gz_each(lambda k: k == r, lambda copy: copy.wait_recv())

    for b in range(2):
        rows = slab(b, 64)
        g = sum_end(6, 1, b)
        f = head[rows, :]
        out = (g - f * jnp.sum(f * g, axis=1, keepdims=True)) / inorm[rows, 0:1]
        gout[rows, :] = out
        gob[slab(2 * c + b, 64), :] = out.astype(BF)
        share(10, gob, b)

    def tg_copy(r):
        return remote(
            tgy.at[pl.ds(64 * r, 64)], tgr.at[slab(y // 2, 64)], tg_ss.at[r], tg_rs.at[y // 2], ring_y(holders[r])
        )

    def tg_send(r):
        net.wait(("gz", r))
        rows = pl.ds(64 * r, 64)
        own = tgs[slab(4 + r - 2 * kk, 64), :].astype(F32)
        total = (own + from_next[rows, :].astype(F32) + from_last[rows, :].astype(F32)).astype(BF)
        tgy[rows, :] = total

        @pl.when(other(holders[r]))
        def _():
            tg_copy(r).start()

        @pl.when(holders[r] == y)
        def _():
            tgr[slab(y // 2, 64), :] = total

    def tg_sent():
        for r in range(NLO):

            @pl.when(other(holders[r]))
            def _():
                tg_copy(r).wait_send()

    def tg_wait():
        for i in range(4):

            @pl.when(other(takers[i]))
            def _():
                remote(
                    tgy.at[pl.ds(0, 64)], tgr.at[pl.ds(64 * i, 64)], tg_ss.at[0], tg_rs.at[i], pair
                ).wait_recv()

    net.sends.append(tg_sent)
    net.arrivals["tg"] = tg_wait
    tg_send(0)
    for b in range(2):
        net.wait(10 + b)

    def hidden_back(cols):
        g = jnp.dot(gob[...], om[:, cols], preferred_element_type=F32)
        gpre[:, cols] = (g * dgel[:, cols]).astype(BF)

    column_loop(hidden_back)
    tg_send(1)

    def normed_terms(cols):
        part[:, cols] = contract_last(gpre[...], hm[cols, :])

    column_loop(normed_terms)
    core_send(12, 2, 0, 1 - p)
    core_send(12, 2, 1, p)
    core_add(12, 2, 0, 1 - p)
    pair_send(14, 2, 0, 1 - p)
    core_add(12, 2, 1, p)
    tg_send(2)
    tg_send(3)
    xhat, rdev = ln_stats(xp[slab(2 * c + p, 64), :].astype(F32))
    net.wait(14)
    g = (accb[slab(p, 64), :] + er[pl.ds(256, 64), :].astype(F32)) * gperm[...]
    mean_g = jnp.sum(g, axis=1, keepdims=True) * (1.0 / D)
    mean_gx = jnp.sum(g * xhat, axis=1, keepdims=True) * (1.0 / D)
    done = slab(2 * h + c, 64)
    result = (gout[slab(p, 64), :] + rdev * (g - mean_g - xhat * mean_gx)).astype(BF)

    def natural_image(cols):
        out_img[done, cols] = contract_last(result, perm[cols, :]).astype(BF)

    column_loop(natural_image)
    from_far, from_core, from_both = slab(2 * (1 - h) + c, 64), slab(2 * h + 1 - c, 64), slab(2 * (1 - h) + 1 - c, 64)
    swap(15, out_img.at[done], out_img.at[done], far, out_img.at[from_far])
    swap(16, out_img.at[done], out_img.at[done], core, out_img.at[from_core])

    net.wait("tg")
    g = tgr[pl.ds(0, 64), :].astype(F32)
    for k in range(1, 4):
        g = g + tgr[slab(k, 64), :].astype(F32)
    tx = tp[...].astype(F32)
    text_norm = jnp.sqrt(jnp.sum(tx * tx, axis=1, keepdims=True) + EPS)
    text_f = tx / text_norm
    g = (g - text_f * jnp.sum(text_f * g, axis=1, keepdims=True)) / text_norm
    high = g.astype(BF)
    both = jnp.concatenate([high, (g - high.astype(F32)).astype(BF)], axis=0)

    def natural_text(cols):
        got = contract_last(both, perm[cols, :])
        out_text[:, cols] = got[:64] + got[64:]

    column_loop(natural_text)
    net.wait(15)
    swap(17, out_img.at[from_far], out_img.at[from_far], core, out_img.at[from_both])


def kernel(*refs):
    net = Net()
    stages(net, *refs)
    net.drain()


def feature_order():
    first = (np.arange(NX * NZ) * (MAIN + REST))[:, None]
    main = (first + np.arange(MAIN)).reshape(-1)
    rest = (first + MAIN + np.arange(REST)).reshape(-1)
    return np.concatenate([main, rest]).reshape(1, D).astype(np.int32)


def shards(images, layer_norm_gain, hidden_weight, output_weight, text):

    def vm(rows, cols, kind=BF):
        return pltpu.VMEM((rows, cols), kind)

    dma = pltpu.SemaphoreType.DMA
    scratch = [
        vm(16, 2 * FW), vm(64, 2 * FW), vm(D, FW), vm(D, FW), vm(512, 640),
        vm(256, D), vm(256, D), vm(D, D), vm(256, D), vm(1, D, F32),
        vm(256, FW), vm(256, FW, F32), vm(256, FW, F32), vm(256, D, F32),
        vm(384, D), vm(384, D), vm(320, D), vm(320, D),
        vm(256, D), vm(128, D, F32), vm(128, 128, F32), vm(128, D, F32), vm(256, D), vm(256, FW),
        vm(640, D), vm(192, D), vm(640, D), vm(256, D), vm(256, D), vm(256, D), vm(256, D), vm(256, 640), vm(640, 256), vm(128, D, F32), vm(64, D),
        dma((4,)), dma((4,)), dma((2,)), dma((2,)),
        dma((2, 2)), dma((2, 2)), dma((4, 4, 2)), dma((4, 4, 2)),
        dma((2, 4, 2)), dma((2, 4, 2)), dma((2, 8, 2, 2)), dma((2, 8, 2, 2)),
        dma((2,)), dma((2,)), dma((4, 3)), dma((9,)), dma((2, 4)), dma((2, 4)), dma((4,)), dma((4,)), dma((18,)), dma((18,)),
    ]
    vmem = pl.BlockSpec(memory_space=pltpu.VMEM)
    images_gradient, grad_text = pl.pallas_call(
        kernel,
        out_shape=(jax.ShapeDtypeStruct((256, D), BF), jax.ShapeDtypeStruct((64, D), F32)),
        in_specs=[vmem] * 6,
        out_specs=(vmem, vmem),
        scratch_shapes=scratch,
        compiler_params=pltpu.CompilerParams(
            collective_id=0, has_side_effects=True, vmem_limit_bytes=56 * 2**20
        ),
        cost_estimate=pl.CostEstimate(flops=4 * 10**9, bytes_accessed=4 * 10**6, transcendentals=10**6),
    )(images, layer_norm_gain, hidden_weight, output_weight, text, jnp.asarray(feature_order()))
    return images_gradient.astype(F32), grad_text


def solution(mesh):
    placed = (P("dp", None), P(), P("dp", "tensor"), P("tensor", "dp"), P(("dp", "tensor"), None))
    return jax.shard_map(
        shards,
        mesh=mesh,
        in_specs=placed,
        out_specs=(P("dp", None), P(("dp", "tensor"), None)),
        check_vma=False,
    )
```

time: 147 us -> 133 us (0.905)
  the two profiles are of different devices: /device:TPU:25 before, /device:TPU:9 now
where the time goes in v3:
time: 133 us
  Pallas kernels  128 us (96%)
  local copies, waits for them, and re-layouts  2.37 us (2%)
  other arithmetic  2.2 us (2%)
    pallas_call x1, Pallas kernels, shards(): pl.pallas_call(kernel, out_shape=(jax.ShapeDtypeStruct((256, D), BF), jax...  128 us

profile of v3, /device:TPU:9, one launch (start us, length us, event | category | flops | bytes accessed | tf_op | source)
XLA Modules:
  0.0 132.7 jit_solution(12401837439041761914)
XLA Ops:
  0.6 1.7 %copy.8.refs_3_ = bf16[1076,9]{1,0:T(8,128)(2,1)} copy(bf16[1076,9]{0,1:T(8,128)(2,1)} %param.9) | data formatting | bytes 38736 | tf_op args[3]
  2.3 127.5 %shard_map.77 = (bf16[256,1152]{1,0:T(8,128)(2,1)}, f32[64,1152]{1,0:T(8,128)}) custom-call(bf16[256,1152]{1,0:T(8,128)(2,1)} %refs_0_.1, f32[1152]{0:T(1024)} %refs_1_.1, bf16[9,1076]{1,0:T(8,128)(2,1)} %refs_2_.1, bf16[1076,9]{1,0:T(8,128)(2,1)} %copy.8.refs_3_, bf16[64,1152]{1,0:T(8,128)(2,1)} %refs_4_.1, s32[1,1152]{1,0:T(1,128)} %constant.2.clone.refs_5_), custom_call_target="tpu_custom_call" | custom-call | flops 4000000000 | bytes 4000000 | tf_op jit(solution)/shard_map/pallas_call | solution.py:664
  129.8 0.0 copy-start
  129.8 2.2 %convert_element_type.3 = f32[256,1152]{1,0:T(8,128)} convert(bf16[256,1152]{1,0:T(8,128)(2,1)} %get-tuple-element.4) | non-fusion elementwise | flops 294912 | bytes 1769472 | tf_op jit(solution)/shard_map/convert_element_type | solution.py:675
  132.0 0.0 copy-done
  132.0 0.7 copy.10
Async XLA Ops:
  129.8 2.2 %copy-start = (f32[64,1152]{1,0:T(8,128)S(1)}, f32[64,1152]{1,0:T(8,128)}, u32[]{:S(2)}) copy-start(f32[64,1152]{1,0:T(8,128)} %get-tuple-element.9) | copy-start | bytes 884740

commit v4 on v3

--- a/solution.py
+++ b/solution.py
@@ -16,6 +16,7 @@
 MAIN, REST = 32, 4
 FOLDS = ((0, 640), (640, 512), (1152, 640), (1792, 512))
 OWN = 9
+SPANS = ((0, FW), (FW, 256))
 ARRIVALS = (
     ("Az", 0, 1), ("Bx", 0, 1), ("Bz", 0, 1), ("Ax", 0, 1), ("Bx", 0, 2), ("Az", 0, 2), ("Bx", -1, 1), ("Bz", 0, 2),
     ("Az", -1, 1), ("Bx", 1, 1), ("Ax", 0, 2), ("Az", 1, 1), ("Bx", -1, 2), ("Az", 0, 3), ("Bx", -2, 1), ("Bz", 0, 3),
@@ -38,6 +39,32 @@
     return (x * (NZ * NLO) + z * NLO + lax.rem(y, NLO), (y // NLO) * 2 + c)
 
 
+ROUTES = {
+    (0, 0): ((4,), ()),
+    (0, 1): ((), (6, 4, 2)),
+    (0, 2): ((2, 4, 6), ()),
+    (1, 0): ((4,), (0,)),
+    (1, 1): ((2,), (0, 6, 4)),
+    (1, 2): ((2,), (6,)),
+    (2, 0): ((), (0, 6, 4)),
+    (2, 1): ((4, 6, 0), ()),
+    (2, 2): ((6,), ()),
+    (3, 0): ((4,), (2, 0, 6)),
+    (3, 1): ((4, 6), (2, 0)),
+    (4, 0): ((5,), (1,)),
+    (4, 1): ((5,), (3, 1, 7)),
+    (4, 2): ((5, 7), (3, 1)),
+    (5, 0): ((1,), ()),
+    (5, 1): ((), (3, 1, 7)),
+    (5, 2): ((7,), (3,)),
+    (6, 0): ((7, 1), (5, 3)),
+    (6, 1): ((7, 1, 3), (5,)),
+    (6, 2): ((7,), (3,)),
+    (7, 0): ((1, 3), (5,)),
+    (7, 1): ((1, 3), (5,)),
+}
+
+
 class Net:
     def __init__(self):
         self.sends, self.arrivals = [], {}
@@ -120,10 +147,10 @@
 def stages(
     net, images, gain_in, h_in, o_in, text, order,
     out_img, out_text,
-    w_own, wy, hm, om, rest, xin, xp, perm, npm, gperm, act, preact, dgel, part,
+    w_own, o_own, wy, wo, stack, hm, om, rest, xin, xp, perm, npm, gperm, act, preact, dgel, part,
     cs, cr, es, er, unit, head, inorm, gout, gob, gpre, texts, tz, tgs, from_next, from_last, tgy, tgr, slopes, slopes_t, accb, tp,
     y_ss, y_rs, im_ss, im_rs, ax_ss, ax_rs, az_ss, az_rs, bz_ss, bz_rs, bx_ss, bx_rs,
-    tz_ss, tz_rs, tx_ss, tx_rs, gz_ss, gz_rs, tg_ss, tg_rs, sw_ss, sw_rs,
+    tz_ss, tz_rs, tx_ss, tf_ss, tx_rs, gz_ss, gz_rs, tg_ss, tg_rs, sw_ss, sw_rs,
 ):
     a = lax.axis_index("dp")
     t = lax.axis_index("tensor")
@@ -179,16 +206,22 @@
     from_last[...] = jnp.zeros((256, D), BF)
     width = h_in.shape[1]
     turn = pick_matrix(16, OWN, [lambda row, col: row == col])
-    w_own[...] = jnp.zeros((16, 2 * FW), BF)
+    w_own[...] = jnp.zeros((16, FW + 256), BF)
     w_own[pl.ds(0, OWN), pl.ds(0, width)] = h_in[...]
-    w_own[:, pl.ds(FW, width)] = contract_last(turn, o_in[...]).astype(BF)
+    o_own[...] = jnp.zeros((16, FW), BF)
+    o_own[:, pl.ds(0, width)] = contract_last(turn, o_in[...]).astype(BF)
+    w_own[:, pl.ds(FW, 256)] = o_own[:, pl.ds(0, 256)]
+    for u in range(7):
+        for v in range(OWN):
+            w_own[pl.ds(OWN + u, 1), pl.ds(128 * v, 128)] = o_own[pl.ds(v, 1), pl.ds(256 + 128 * u, 128)]
 
     bar = pltpu.get_barrier_semaphore()
 
     def signal(device):
         pl.semaphore_signal(bar, inc=1, device_id=device, device_id_type=MESH)
 
-    for device in (core, pair, far, x_up, x_dn, z_up, z_dn, last, after):
+    beyond = (ring_y(lax.rem(y + 2, NY)), ring_y(lax.rem(y + NY - 2, NY)))
+    for device in (core, pair, far, x_up, x_dn, z_up, z_dn, last, after, *beyond):
         signal(device)
     for k in takers + holders:
 
@@ -196,37 +229,45 @@
         def _():
             signal(ring_y(k))
 
-    pl.semaphore_wait(bar, 17 - 2 * mine.astype(jnp.int32))
-
-    def y_copy(i):
-        return remote(w_own, wy.at[slab(lo, 16)], y_ss.at[i], y_rs.at[lo], ring_y(takers[i]))
+    pl.semaphore_wait(bar, 19 - 2 * mine.astype(jnp.int32))
+
+    def half(ref, n):
+        return ref.at[:, pl.ds(*SPANS[n])]
+
+    def y_copy(n, i):
+        to = wy.at[slab(lo, 16), pl.ds(*SPANS[n])]
+        return remote(half(w_own, n), to, y_ss.at[n, i], y_rs.at[n, lo], ring_y(takers[i]))
 
     def y_sent():
+        for n in range(2):
+            for i in range(4):
+
+                @pl.when(other(takers[i]))
+                def _():
+                    y_copy(n, i).wait_send()
+
+    def y_wait(n):
+        for l in range(NLO):
+
+            @pl.when(other(holders[l]))
+            def _():
+                came = wy.at[slab(l, 16), pl.ds(*SPANS[n])]
+                remote(half(w_own, n), came, y_ss.at[n, 0], y_rs.at[n, l], pair).wait_recv()
+
+    for n in range(2):
         for i in range(4):
 
             @pl.when(other(takers[i]))
             def _():
-                y_copy(i).wait_send()
-
-    def y_wait():
-        for l in range(NLO):
-
-            @pl.when(other(holders[l]))
+                y_copy(n, i).start()
+
+            @pl.when(takers[i] == y)
             def _():
-                remote(w_own, wy.at[slab(l, 16)], y_ss.at[0], y_rs.at[l], pair).wait_recv()
-
-    for i in range(4):
-
-        @pl.when(other(takers[i]))
-        def _():
-            y_copy(i).start()
-
-        @pl.when(takers[i] == y)
-        def _():
-            wy[slab(lo, 16), :] = w_own[...]
+                wy[slab(lo, 16), pl.ds(*SPANS[n])] = w_own[:, pl.ds(*SPANS[n])]
 
     net.sends.append(y_sent)
-    net.arrivals["y"] = y_wait
+    net.arrivals["y", 0] = lambda: y_wait(0)
+    net.arrivals["y", 1] = lambda: y_wait(1)
 
     @pl.loop(0, 9)
     def _(k):
@@ -256,44 +297,70 @@
             remote(mine_tz, here, tz_ss.at[d], tz_rs.at[d], back),
         )
 
-    def text_slot(i, d):
-        k = i % 2
-        used = {(0, 2): lo == 0, (1, 0): lo >= 2, (1, 2): lo <= 2}.get((k, d), True)
-        return 4 * d + lo - 2 * k, used
-
-    def tx_copy(i, d):
-        j, _ = text_slot(i, d)
-        return remote(
-            tz.at[pl.ds(64 * d, 64)], texts.at[slab(j, 64)], tx_ss.at[i, d], tx_rs.at[j], ring_y(takers[i])
-        )
-
-    def tx_send(i, d):
-        j, used = text_slot(i, d)
-
-        @when(used, other(takers[i]))
-        def _():
-            tx_copy(i, d).start()
-
-        @when(used, takers[i] == y)
-        def _():
-            texts[slab(j, 64), :] = tz[pl.ds(64 * d, 64), :]
+    def text_slot(to, source, d):
+        return 4 * d + source % NLO - (to % NLO) // 2 * 2
+
+    def each_text(act):
+        for (source, d), ways in ROUTES.items():
+            for way in (0, 1):
+                stops = (source, *ways[way])
+                for hop in range(len(stops) - 1):
+                    act(d, stops[hop], hop, way, source, stops[hop + 1])
+
+    def tx_copy(d, at, hop, way, source, to):
+        if hop == 0:
+            src, sem = tz.at[pl.ds(64 * d, 64)], tx_ss.at[d, way]
+        else:
+            j = text_slot(at, source, d)
+            src, sem = texts.at[pl.ds(64 * j, 64)], tf_ss.at[j]
+        j = text_slot(to, source, d)
+        return remote(src, texts.at[pl.ds(64 * j, 64)], sem, tx_rs.at[j], ring_y(jnp.int32(to)))
+
+    def tx_came(j):
+        remote(tz.at[pl.ds(64, 64)], texts.at[pl.ds(64 * j, 64)], tx_ss.at[0, 0], tx_rs.at[j], pair).wait_recv()
+
+    passing = set()
+    each_text(lambda d, at, hop, way, source, to: hop and passing.add((at, text_slot(at, source, d))))
+
+    def tx_send(depth, column):
+        def act(d, at, hop, way, source, to):
+            if (hop, d) == (depth, column):
+
+                @pl.when(y == at)
+                def _():
+                    if hop:
+                        tx_came(text_slot(at, source, d))
+                    tx_copy(d, at, hop, way, source, to).start()
+
+        each_text(act)
+
+    def tx_keep(d):
+        for at in range(NY):
+            j = text_slot(at, at, d)
+            if at // NLO == at % 2 and 0 <= j <= 8:
+
+                @pl.when(y == at)
+                def _():
+                    texts[pl.ds(64 * j, 64), :] = tz[pl.ds(64 * d, 64), :]
 
     def tx_sent():
-        for d in range(3):
-            for i in range(4):
-
-                @when(text_slot(i, d)[1], other(takers[i]))
-                def _():
-                    tx_copy(i, d).wait_send()
+        def act(*hop):
+            @pl.when(y == hop[1])
+            def _():
+                tx_copy(*hop).wait_send()
+
+        each_text(act)
 
     def tx_wait():
         for j in range(9):
-
-            @when(jnp.logical_not(mine & (p == j % 4)))
+            done = mine & (p == j % 4)
+            for at in range(NY):
+                if (at, j) in passing:
+                    done = done | (y == at)
+
+            @pl.when(jnp.logical_not(done))
             def _():
-                remote(
-                    tz.at[pl.ds(64, 64)], texts.at[slab(j, 64)], tx_ss.at[0, 0], tx_rs.at[j], pair
-                ).wait_recv()
+                tx_came(j)
 
     net.sends.append(tx_sent)
     net.arrivals["tx"] = tx_wait
@@ -337,22 +404,31 @@
         for one in rings[key]:
             one.send(1)
 
-    net.wait("y")
+    net.wait(("y", 0))
     keep = pick_matrix(MAIN, 64, [lambda row, col: row == lax.shift_right_logical(col, 4) * OWN + (col & 15)])
     keep = jnp.where((lax.broadcasted_iota(jnp.int32, (MAIN, 64), 1) & 15) < OWN, keep, jnp.zeros_like(keep))
     mine_main = pl.ds(pl.multiple_of(place(x, z, MAIN), MAIN), MAIN)
     hm[mine_main, :] = jnp.dot(keep, wy[:, pl.ds(0, FW)], preferred_element_type=F32).astype(BF)
     begin(("Az", 0))
-    om[mine_main, :] = jnp.dot(keep, wy[:, pl.ds(FW, FW)], preferred_element_type=F32).astype(BF)
+    begin(("Ax", 0))
+    for v in range(OWN):
+        stack[pl.ds(64 * v, 64), :] = wy[:, pl.ds(128 * v, 128)]
+    for u in range(7):
+        pick = pick_matrix(64, 64 * OWN, [lambda row, col: col == (row & 15) * 64 + (row & 48) + OWN + u])
+        wo[:, pl.ds(256 + 128 * u, 128)] = jnp.dot(pick, stack[...], preferred_element_type=F32).astype(BF)
+    net.wait(("y", 1))
+    wo[:, pl.ds(0, 256)] = wy[:, pl.ds(FW, 256)]
+    om[mine_main, :] = jnp.dot(keep, wo[...], preferred_element_type=F32).astype(BF)
     folded = jnp.zeros((16, 640), F32)
     for u, (lane, lanes) in enumerate(FOLDS):
         pick = pick_matrix(16, 64, [lambda row, col: ((row & 3) == u) & (col == 48 + 5 + lax.shift_right_logical(row, 2))])
-        got = jnp.dot(pick, wy[:, pl.ds(lane, lanes)], preferred_element_type=F32)
+        held = wy[:, pl.ds(lane, lanes)] if lane < FW else wo[:, pl.ds(lane - FW, lanes)]
+        got = jnp.dot(pick, held, preferred_element_type=F32)
         if lanes < 640:
             got = jnp.concatenate([got, jnp.zeros((16, 640 - lanes), F32)], axis=1)
         folded = folded + got
     rest[pl.ds(pl.multiple_of(place(x, z, 16), 16), 16), :] = folded.astype(BF)
-    for key in (("Bz", 0), ("Bx", 0), ("Ax", 0)):
+    for key in (("Bz", 0), ("Bx", 0)):
         begin(key)
 
     def im_copy(k, block):
@@ -364,9 +440,15 @@
         net.start(im_copy(k, p), ("im", k), im_copy(k, 1 - p))
         xin[slab(2 * k + p, 64), :] = images[slab(2 * h + k, 64), :]
 
-    sends = [lambda i=i: tx_send(i, 1) for i in range(4)]
-    sends += [lambda: net.wait(("tz", 0)), lambda: net.wait(("tz", 1))]
-    sends += [lambda i=i, d=d: tx_send(i, d) for d in (0, 2) for i in range(4)]
+    def text_start(d):
+        if d != 1:
+            net.wait(("tz", d // 2))
+        tx_send(0, d)
+        tx_keep(d)
+
+    beside = {0: lambda: text_start(1), 4: lambda: text_start(0), 5: lambda: text_start(2)}
+    for n, hop in ((20, (1, 1)), (24, (1, 0)), (26, (1, 2)), (31, (2, 1)), (34, (2, 0)), (36, (2, 2))):
+        beside[n] = lambda hop=hop: tx_send(*hop)
 
     def normed_rows():
         for k in range(2):
@@ -391,8 +473,8 @@
         if route == "Bz":
             for k in (-step, step) if step < 4 else (4,):
                 begin(("Bx", k))
-        if n % 2 == 0 and sends:
-            sends.pop(0)()
+        if n in beside:
+            beside[n]()
         if n == 30:
             normed_rows()
 
@@ -437,9 +519,10 @@
         es[rows, :] = accb[slab(b, 64), :].astype(BF)
         swap(n + at, es.at[rows], er.at[rows], pair)
 
-    def sum_start(n, k):
+    def sum_start(n, k, beside=lambda: None):
         for b in range(2):
             core_send(n, k, b, b)
+        beside()
         for b in range(2):
             core_add(n, k, b, b)
             pair_send(n + 2, k, b, b)
@@ -494,35 +577,90 @@
         part[:, cols] = jnp.dot(slopes[...], texts[:, cols], preferred_element_type=F32)
 
     column_loop(to_image)
-    sum_start(6, 1)
-
-    @pl.loop(0, 5)
-    def _(k):
-        rows = slab(k, 128)
-        row = lax.broadcasted_iota(jnp.int32, (128, 256), 1)
-        col = lax.broadcasted_iota(jnp.int32, (128, 256), 0) + k * 128
-        slopes_t[rows, :] = slope(contract_last(texts[rows, :], unit[...]), row, col)
-
-    def to_text(cols):
-        tgs[:, cols] = jnp.dot(slopes_t[...], unit[:, cols], preferred_element_type=F32).astype(BF)
-
-    column_loop(to_text)
+
+    def text_slopes():
+        @pl.loop(0, 5)
+        def _(k):
+            rows = slab(k, 128)
+            row = lax.broadcasted_iota(jnp.int32, (128, 256), 1)
+            col = lax.broadcasted_iota(jnp.int32, (128, 256), 0) + k * 128
+            slopes_t[rows, :] = slope(contract_last(texts[rows, :], unit[...]), row, col)
+
+    sum_start(6, 1, text_slopes)
+
+    def gz_part(k, d, r):
+        device, buf = ((last, from_next), (after, from_last))[d]
+        there = buf.at[pl.ds(64 * r, 64)]
+        j = 8 * d + r - 2 * k
+        return remote(tgs.at[pl.ds(64 * j, 64)], there, gz_ss.at[d, r], gz_rs.at[d, r], device)
+
+    gz_parts = [(k, d, r) for k in range(2) for d in range(2) for r in range(NLO) if 0 <= 8 * d + r - 2 * k <= 8]
+
     def gz_each(pick, act):
+        for k, d, r in gz_parts:
+            if pick(8 * d + r - 2 * k):
+
+                @pl.when(kk == k)
+                def _():
+                    act(gz_part(k, d, r))
+
+    for k in (0, 4, 1, 3, 2):
+        rows = pl.ds(128 * k, 128)
+
+        def to_text(cols):
+            tgs[rows, cols] = jnp.dot(slopes_t[rows, :], unit[:, cols], preferred_element_type=F32).astype(BF)
+
+        column_loop(to_text)
+        gz_each(lambda j: j // 2 == k, lambda copy: copy.start())
+    net.sends.append(lambda: gz_each(lambda j: True, lambda copy: copy.wait_send()))
+
+    def tg_copy(r):
+        return remote(
+            tgy.at[pl.ds(64 * r, 64)], tgr.at[slab(y // 2, 64)], tg_ss.at[r], tg_rs.at[y // 2], ring_y(holders[r])
+        )
+
+    def tg_send(n):
         for k in range(2):
-            for d, device, buf in ((0, last, from_next), (1, after, from_last)):
-                for r in range(NLO):
-                    j = 8 * d + r - 2 * k
-                    if 0 <= j <= 8 and pick(r):
-
-                        @pl.when(kk == k)
-                        def _():
-                            there = buf.at[pl.ds(64 * r, 64)]
-                            act(remote(tgs.at[pl.ds(64 * j, 64)], there, gz_ss.at[d, r], gz_rs.at[d, r], device))
-
-    gz_each(lambda r: True, lambda copy: copy.start())
-    net.sends.append(lambda: gz_each(lambda r: True, lambda copy: copy.wait_send()))
-    for r in range(NLO):
-        net.arrivals["gz", r] = lambda r=r: gz_each(lambda k: k == r, lambda copy: copy.wait_recv())
+
+            @pl.when(kk == k)
+            def _():
+                tg_row(k, (n + 2 * k) % NLO)
+
+    def tg_row(k, r):
+        for part in gz_parts:
+            if part[0] == k and part[2] == r:
+                gz_part(*part).wait_recv()
+        rows = pl.ds(64 * r, 64)
+        own = tgs[pl.ds(64 * (4 + r - 2 * k), 64), :].astype(F32)
+        total = (own + from_next[rows, :].astype(F32) + from_last[rows, :].astype(F32)).astype(BF)
+        tgy[rows, :] = total
+
+        @pl.when(other(holders[r]))
+        def _():
+            tg_copy(r).start()
+
+        @pl.when(holders[r] == y)
+        def _():
+            tgr[slab(y // 2, 64), :] = total
+
+    def tg_sent():
+        for r in range(NLO):
+
+            @pl.when(other(holders[r]))
+            def _():
+                tg_copy(r).wait_send()
+
+    def tg_wait():
+        for i in range(4):
+
+            @pl.when(other(takers[i]))
+            def _():
+                remote(
+                    tgy.at[pl.ds(0, 64)], tgr.at[pl.ds(64 * i, 64)], tg_ss.at[0], tg_rs.at[i], pair
+                ).wait_recv()
+
+    tg_send(0)
+    tg_send(1)
 
     for b in range(2):
         rows = slab(b, 64)
@@ -533,45 +671,9 @@
         gob[slab(2 * c + b, 64), :] = out.astype(BF)
         share(10, gob, b)
 
-    def tg_copy(r):
-        return remote(
-            tgy.at[pl.ds(64 * r, 64)], tgr.at[slab(y // 2, 64)], tg_ss.at[r], tg_rs.at[y // 2], ring_y(holders[r])
-        )
-
-    def tg_send(r):
-        net.wait(("gz", r))
-        rows = pl.ds(64 * r, 64)
-        own = tgs[slab(4 + r - 2 * kk, 64), :].astype(F32)
-        total = (own + from_next[rows, :].astype(F32) + from_last[rows, :].astype(F32)).astype(BF)
-        tgy[rows, :] = total
-
-        @pl.when(other(holders[r]))
-        def _():
-            tg_copy(r).start()
-
-        @pl.when(holders[r] == y)
-        def _():
-            tgr[slab(y // 2, 64), :] = total
-
-    def tg_sent():
-        for r in range(NLO):
-
-            @pl.when(other(holders[r]))
-            def _():
-                tg_copy(r).wait_send()
-
-    def tg_wait():
-        for i in range(4):
-
-            @pl.when(other(takers[i]))
-            def _():
-                remote(
-                    tgy.at[pl.ds(0, 64)], tgr.at[pl.ds(64 * i, 64)], tg_ss.at[0], tg_rs.at[i], pair
-                ).wait_recv()
-
     net.sends.append(tg_sent)
     net.arrivals["tg"] = tg_wait
-    tg_send(0)
+    tg_send(2)
     for b in range(2):
         net.wait(10 + b)
 
@@ -580,7 +682,7 @@
         gpre[:, cols] = (g * dgel[:, cols]).astype(BF)
 
     column_loop(hidden_back)
-    tg_send(1)
+    tg_send(3)
 
     def normed_terms(cols):
         part[:, cols] = contract_last(gpre[...], hm[cols, :])
@@ -591,8 +693,6 @@
     core_add(12, 2, 0, 1 - p)
     pair_send(14, 2, 0, 1 - p)
     core_add(12, 2, 1, p)
-    tg_send(2)
-    tg_send(3)
     xhat, rdev = ln_stats(xp[slab(2 * c + p, 64), :].astype(F32))
     net.wait(14)
     g = (accb[slab(p, 64), :] + er[pl.ds(256, 64), :].astype(F32)) * gperm[...]
@@ -649,16 +749,16 @@
 
     dma = pltpu.SemaphoreType.DMA
     scratch = [
-        vm(16, 2 * FW), vm(64, 2 * FW), vm(D, FW), vm(D, FW), vm(512, 640),
+        vm(16, FW + 256), vm(16, FW), vm(64, FW + 256), vm(64, FW), vm(64 * OWN, 128), vm(D, FW), vm(D, FW), vm(512, 640),
         vm(256, D), vm(256, D), vm(D, D), vm(256, D), vm(1, D, F32),
         vm(256, FW), vm(256, FW, F32), vm(256, FW, F32), vm(256, D, F32),
         vm(384, D), vm(384, D), vm(320, D), vm(320, D),
         vm(256, D), vm(128, D, F32), vm(128, 128, F32), vm(128, D, F32), vm(256, D), vm(256, FW),
         vm(640, D), vm(192, D), vm(640, D), vm(256, D), vm(256, D), vm(256, D), vm(256, D), vm(256, 640), vm(640, 256), vm(128, D, F32), vm(64, D),
-        dma((4,)), dma((4,)), dma((2,)), dma((2,)),
+        dma((2, 4)), dma((2, 4)), dma((2,)), dma((2,)),
         dma((2, 2)), dma((2, 2)), dma((4, 4, 2)), dma((4, 4, 2)),
         dma((2, 4, 2)), dma((2, 4, 2)), dma((2, 8, 2, 2)), dma((2, 8, 2, 2)),
-        dma((2,)), dma((2,)), dma((4, 3)), dma((9,)), dma((2, 4)), dma((2, 4)), dma((4,)), dma((4,)), dma((18,)), dma((18,)),
+        dma((2,)), dma((2,)), dma((3, 2)), dma((9,)), dma((9,)), dma((2, 4)), dma((2, 4)), dma((4,)), dma((4,)), dma((18,)), dma((18,)),
     ]
     vmem = pl.BlockSpec(memory_space=pltpu.VMEM)
     images_gradient, grad_text = pl.pallas_call(

time: 133 us -> 129 us (0.970)
  the two profiles are of different devices: /device:TPU:9 before, /device:TPU:33 now
where the time goes in v4:
time: 129 us
  Pallas kernels  124 us (96%)
  local copies, waits for them, and re-layouts  2.37 us (2%)
  other arithmetic  2.2 us (2%)
    pallas_call x1, Pallas kernels, shards(): pl.pallas_call(kernel, out_shape=(jax.ShapeDtypeStruct((256, D), BF), jax...  124 us

profile of v4, /device:TPU:33, one launch (start us, length us, event | category | flops | bytes accessed | tf_op | source)
XLA Modules:
  0.0 129.0 jit_solution(9634837443193330486)
XLA Ops:
  0.6 1.7 %copy.8.refs_3_ = bf16[1076,9]{1,0:T(8,128)(2,1)} copy(bf16[1076,9]{0,1:T(8,128)(2,1)} %param.9) | data formatting | bytes 38736 | tf_op args[3]
  2.3 123.8 %shard_map.77 = (bf16[256,1152]{1,0:T(8,128)(2,1)}, f32[64,1152]{1,0:T(8,128)}) custom-call(bf16[256,1152]{1,0:T(8,128)(2,1)} %refs_0_.1, f32[1152]{0:T(1024)} %refs_1_.1, bf16[9,1076]{1,0:T(8,128)(2,1)} %refs_2_.1, bf16[1076,9]{1,0:T(8,128)(2,1)} %copy.8.refs_3_, bf16[64,1152]{1,0:T(8,128)(2,1)} %refs_4_.1, s32[1,1152]{1,0:T(1,128)} %constant.2.clone.refs_5_), custom_call_target="tpu_custom_call" | custom-call | flops 4000000000 | bytes 4000000 | tf_op jit(solution)/shard_map/pallas_call | solution.py:764
  126.1 0.0 copy-start
  126.1 2.2 %convert_element_type.3 = f32[256,1152]{1,0:T(8,128)} convert(bf16[256,1152]{1,0:T(8,128)(2,1)} %get-tuple-element.4) | non-fusion elementwise | flops 294912 | bytes 1769472 | tf_op jit(solution)/shard_map/convert_element_type | solution.py:775
  128.3 0.0 copy-done
  128.3 0.7 copy.10
Async XLA Ops:
  126.1 2.2 %copy-start = (f32[64,1152]{1,0:T(8,128)S(1)}, f32[64,1152]{1,0:T(8,128)}, u32[]{:S(2)}) copy-start(f32[64,1152]{1,0:T(8,128)} %get-tuple-element.9) | copy-start | bytes 884740

commit v5 on v4

--- a/solution.py
+++ b/solution.py
@@ -146,9 +146,9 @@
 
 def stages(
     net, images, gain_in, h_in, o_in, text, order,
-    out_img, out_text,
+    out_full, out_text,
     w_own, o_own, wy, wo, stack, hm, om, rest, xin, xp, perm, npm, gperm, act, preact, dgel, part,
-    cs, cr, es, er, unit, head, inorm, gout, gob, gpre, texts, tz, tgs, from_next, from_last, tgy, tgr, slopes, slopes_t, accb, tp,
+    cs, cr, es, er, unit, head, inorm, gout, gob, gpre, texts, tz, tgs, from_next, from_last, tgy, tgr, slopes, slopes_t, accb, tp, out_img,
     y_ss, y_rs, im_ss, im_rs, ax_ss, ax_rs, az_ss, az_rs, bz_ss, bz_rs, bx_ss, bx_rs,
     tz_ss, tz_rs, tx_ss, tf_ss, tx_rs, gz_ss, gz_rs, tg_ss, tg_rs, sw_ss, sw_rs,
 ):
@@ -447,7 +447,7 @@
         tx_keep(d)
 
     beside = {0: lambda: text_start(1), 4: lambda: text_start(0), 5: lambda: text_start(2)}
-    for n, hop in ((20, (1, 1)), (24, (1, 0)), (26, (1, 2)), (31, (2, 1)), (34, (2, 0)), (36, (2, 2))):
+    for n, hop in ((24, (1, 1)), (28, (1, 0)), (30, (1, 2)), (35, (2, 1)), (36, (2, 0)), (37, (2, 2))):
         beside[n] = lambda hop=hop: tx_send(*hop)
 
     def normed_rows():
@@ -733,6 +733,7 @@
     net = Net()
     stages(net, *refs)
     net.drain()
+    refs[6][...] = refs[46][...].astype(F32)
 
 
 def feature_order():
@@ -754,16 +755,16 @@
         vm(256, FW), vm(256, FW, F32), vm(256, FW, F32), vm(256, D, F32),
         vm(384, D), vm(384, D), vm(320, D), vm(320, D),
         vm(256, D), vm(128, D, F32), vm(128, 128, F32), vm(128, D, F32), vm(256, D), vm(256, FW),
-        vm(640, D), vm(192, D), vm(640, D), vm(256, D), vm(256, D), vm(256, D), vm(256, D), vm(256, 640), vm(640, 256), vm(128, D, F32), vm(64, D),
+        vm(640, D), vm(192, D), vm(640, D), vm(256, D), vm(256, D), vm(256, D), vm(256, D), vm(256, 640), vm(640, 256), vm(128, D, F32), vm(64, D), vm(256, D),
         dma((2, 4)), dma((2, 4)), dma((2,)), dma((2,)),
         dma((2, 2)), dma((2, 2)), dma((4, 4, 2)), dma((4, 4, 2)),
         dma((2, 4, 2)), dma((2, 4, 2)), dma((2, 8, 2, 2)), dma((2, 8, 2, 2)),
         dma((2,)), dma((2,)), dma((3, 2)), dma((9,)), dma((9,)), dma((2, 4)), dma((2, 4)), dma((4,)), dma((4,)), dma((18,)), dma((18,)),
     ]
     vmem = pl.BlockSpec(memory_space=pltpu.VMEM)
-    images_gradient, grad_text = pl.pallas_call(
+    return pl.pallas_call(
         kernel,
-        out_shape=(jax.ShapeDtypeStruct((256, D), BF), jax.ShapeDtypeStruct((64, D), F32)),
+        out_shape=(jax.ShapeDtypeStruct((256, D), F32), jax.ShapeDtypeStruct((64, D), F32)),
         in_specs=[vmem] * 6,
         out_specs=(vmem, vmem),
         scratch_shapes=scratch,
@@ -772,7 +773,6 @@
         ),
         cost_estimate=pl.CostEstimate(flops=4 * 10**9, bytes_accessed=4 * 10**6, transcendentals=10**6),
     )(images, layer_norm_gain, hidden_weight, output_weight, text, jnp.asarray(feature_order()))
-    return images_gradient.astype(F32), grad_text
 
 
 def solution(mesh):

time: 129 us -> 129 us (level)
  the two profiles are of different devices: /device:TPU:33 before, /device:TPU:37 now
where the time goes in v5:
time: 129 us
  Pallas kernels  123 us (95%)
  local copies, waits for them, and re-layouts  4.78 us (4%)
    pallas_call x1, Pallas kernels, shards(): pl.pallas_call(kernel, out_shape=(jax.ShapeDtypeStruct((256, D), F32), ja...  123 us
    unnamed x5, local copies, waits for them, and re-layouts  4.78 us

profile of v5, /device:TPU:37, one launch (start us, length us, event | category | flops | bytes accessed | tf_op | source)
XLA Modules:
  0.0 128.8 jit_solution(5833822728308924113)
XLA Ops:
  0.6 1.7 %copy.8.refs_3_ = bf16[1076,9]{1,0:T(8,128)(2,1)} copy(bf16[1076,9]{0,1:T(8,128)(2,1)} %param.9) | data formatting | bytes 38736 | tf_op args[3]
  2.3 123.4 %shard_map.77 = (f32[256,1152]{1,0:T(8,128)}, f32[64,1152]{1,0:T(8,128)}) custom-call(bf16[256,1152]{1,0:T(8,128)(2,1)} %refs_0_.1, f32[1152]{0:T(1024)} %refs_1_.1, bf16[9,1076]{1,0:T(8,128)(2,1)} %refs_2_.1, bf16[1076,9]{1,0:T(8,128)(2,1)} %copy.8.refs_3_, bf16[64,1152]{1,0:T(8,128)(2,1)} %refs_4_.1, s32[1,1152]{1,0:T(1,128)} %constant.2.clone.refs_5_), custom_call_target="tpu_custom_call" | custom-call | flops 4000000000 | bytes 4000000 | tf_op jit(solution)/shard_map/pallas_call | solution.py:765
  125.7 0.0 copy-start
  125.7 2.4 %copy.11 = f32[256,1152]{1,0:T(8,128)} copy(f32[256,1152]{1,0:T(8,128)} %get-tuple-element.4) | data formatting | bytes 2359296
  128.1 0.0 copy-done
  128.1 0.7 copy.12
Async XLA Ops:
  125.7 2.4 %copy-start = (f32[64,1152]{1,0:T(8,128)S(1)}, f32[64,1152]{1,0:T(8,128)}, u32[]{:S(2)}) copy-start(f32[64,1152]{1,0:T(8,128)} %get-tuple-element.5) | copy-start | bytes 884740
